TPU v7x, 256 devices: a whole 4x4x8 slice. The times are simulated.
256 devices in a mesh: gx: 16 (over z_lo, x), gy: 4 (over y), gz: 4 (over z_hi, core).
Axes of the slice: x: 4, y: 4, z: 8 (z_hi: 2, z_lo: 4; z = z_hi * 4 + z_lo), core: 2. Of those that a mesh axis runs over, the one named last changes fastest.
Arguments:
- forcing: float32 [3, 256, 32, 512], P(None, 'gx', 'gy', 'gz'), may hold values from -6 to 6
- guess: float32 [3, 256, 32, 512], P(None, 'gx', 'gy', 'gz'), may hold values from -3 to 3
- lame_first: float32 [256, 32, 512], P('gx', 'gy', 'gz'), may hold values from 0.5 to 8
- shear_modulus: float32 [256, 32, 512], P('gx', 'gy', 'gz'), may hold values from 0.5 to 4
Outputs:
- solution: float32 [3, 256, 32, 512], P(None, 'gx', 'gy', 'gz')
- scaled_residual: float32 [3, 256, 32, 512], P(None, 'gx', 'gy', 'gz')
All inputs are finite; a program needn't handle non-finite values.
Results may differ from a plain program's by a relative error of at most 0.0003.
Values sent between devices are 32-bit elements; how exact they have to be, the bound alone decides.
No kernel may reach another device: no remote copies, remote signals or barrier semaphores. Data moves between devices by JAX's collectives and lax.ppermute only.
A program may use at most 64 MiB of HBM per device.

v0:
```python
import itertools

import jax
import jax.numpy as jnp
from jax import lax
from jax.experimental import pallas as pl
from jax.experimental.pallas import tpu as pltpu
from jax.sharding import PartitionSpec as P

AXES = ("gx", "gy", "gz")
REACH = 4
F32 = jnp.float32
LANES = 128
ROWS = 8


def swap_pairs(dims, axis, kind):
    other = (1, 0, 1)[axis]

    def place(spot):
        return (spot[0] * dims[1] + spot[1]) * dims[2] + spot[2]

    pairs = []
    for spot in itertools.product(*(range(size) for size in dims)):
        goal = list(spot)
        mate = (spot[axis] ^ 1) if kind == 0 else ((spot[axis] + 1) ^ 1) - 1
        if 0 <= mate < dims[axis]:
            goal[axis] = mate
        else:
            goal[other] ^= 1
        pairs.append((place(spot), place(goal)))
    return pairs


def iota(shape, dim):
    return lax.broadcasted_iota(jnp.int32, shape, dim)


def half_turn(tile):
    return pltpu.roll(tile, ROWS // 2, 0)


def even(axis):
    return lax.rem(lax.axis_index(axis), 2) == 0


def at_end(axis):
    place = lax.axis_index(axis)
    return jnp.logical_or(place == 0, place == lax.axis_size(axis) - 1)


def fields_of(forcing, guess, lame, shear):
    return [guess.at[c] for c in range(3)] + [forcing.at[c] for c in range(3)] + [lame, shear]


def row_mask(flag):
    low = iota((ROWS, LANES), 0) < ROWS // 2
    return jnp.logical_xor(low, jnp.broadcast_to(flag, low.shape))


X_LAYERS = (4, 4, 4, 3, 3, 3, 4, 4, 4)
X_STARTS = tuple(sum(X_LAYERS[:f]) for f in range(9))
X_TILES = sum(X_LAYERS)


def pack_first(forcing, guess, lame, shear, own, z_near, z_far, y_near, y_far, x_near, x_far):
    fields = fields_of(forcing, guess, lame, shear)
    layers = own.shape[0]
    slot = lax.rem(iota((ROWS, LANES), 1), 16)
    group = lax.div(iota((ROWS, LANES), 1), 16)
    quarter = lax.div(slot, 4)
    edges = []
    for x in range(layers):
        low = jnp.zeros((ROWS, LANES), F32)
        high = low
        for f in range(8):
            tile = fields[f][x]
            low = jnp.where(group == f, pltpu.roll(tile, (16 * f + 4) % LANES, 1), low)
            high = jnp.where(group == f, pltpu.roll(tile, (16 * f + 12) % LANES, 1), high)
        tile = jnp.where(slot < 8, low, high)
        own[x] = tile
        edges.append(tile)
    up_first = even("gz")
    quads = layers // 4
    for q in range(quads):
        up = edges[q]
        down = edges[q]
        for j in range(4):
            tile = edges[q + quads * j]
            up = jnp.where(quarter == j, pltpu.roll(tile, (4 * j - 8) % LANES, 1), up)
            down = jnp.where(quarter == j, pltpu.roll(tile, (4 * j - 4) % LANES, 1), down)
        z_near[q] = jnp.where(up_first, up, down)
        z_far[q] = jnp.where(up_first, down, up)
    keep = row_mask(even("gy"))
    half = layers // 2
    for f in range(8):
        for x in range(half):
            here = fields[f][x]
            there = half_turn(fields[f][x + half])
            y_near[f * half + x] = jnp.where(keep, here, there)
            y_far[f * half + x] = jnp.where(keep, there, here)
    up_first = even("gx")
    for f in range(8):
        count = X_LAYERS[f]
        last = layers - count
        for x in range(count):
            x_near[X_STARTS[f] + x] = fields[f][jnp.where(up_first, last, 0) + x]
            x_far[X_STARTS[f] + x] = fields[f][jnp.where(up_first, 0, last) + x]


def pack_second(own, z_near, z_far, x_near_in, x_far_in, full, x_near, x_far):
    layers = own.shape[0]
    filled = pl.ds(0, X_STARTS[8])
    x_near[filled] = x_near_in[filled]
    x_far[filled] = x_far_in[filled]
    quads = layers // 4
    slot = lax.rem(iota((ROWS, LANES), 1), 16)
    forward = even("gz")
    ends = at_end("gz")
    for q in range(quads):
        near = z_near[q]
        far = jnp.where(ends, 0.0, z_far[q])
        behind = jnp.where(forward, far, near)
        ahead = jnp.where(forward, near, far)
        for j in range(4):
            x = q + quads * j
            tile = jnp.where(slot < 4, pltpu.roll(behind, (-4 * j) % LANES, 1), own[x])
            full[x] = jnp.where(slot >= 12, pltpu.roll(ahead, (12 - 4 * j) % LANES, 1), tile)
    up_first = even("gx")
    last = layers - 4
    for x in range(4):
        x_near[X_STARTS[8] + x] = full[jnp.where(up_first, last, 0) + x]
        x_far[X_STARTS[8] + x] = full[jnp.where(up_first, 0, last) + x]


def pack_third(full, x_near, x_far, y_near, y_far):
    keep = row_mask(even("gy"))
    half = full.shape[0] // 2
    for i in range(X_TILES):
        here = x_near[i]
        there = half_turn(x_far[i])
        y_near[i] = jnp.where(keep, here, there)
        y_far[i] = jnp.where(keep, there, here)
    for x in range(half):
        here = full[x]
        there = half_turn(full[x + half])
        y_near[X_TILES + x] = jnp.where(keep, here, there)
        y_far[X_TILES + x] = jnp.where(keep, there, here)


def row_next(tile):
    return pltpu.roll(tile, tile.shape[0] - 1, 0)


def row_prev(tile):
    return pltpu.roll(tile, 1, 0)


def lane_next(tile):
    return pltpu.roll(tile, LANES - 1, 1)


def lane_prev(tile):
    return pltpu.roll(tile, 1, 1)


def node_modes(here, beyond):
    total = here + beyond
    change = beyond - here
    total_y = row_next(total)
    change_y = row_next(change)
    return (total + total_y, total_y - total, change + change_y, change_y - change)


def element_modes(lower, upper, lam, mu):
    s = [[lower[c][m] + upper[c][m] for m in range(4)] for c in range(3)]
    d = [[upper[c][m] - lower[c][m] for m in range(4)] for c in range(3)]
    mu2 = mu + mu
    lam3 = lam * (1.0 / 3.0)
    mu3 = mu * (1.0 / 3.0)
    stiff = (lam3 + 4.0 * mu3) * (1.0 / 3.0)
    pressure = lam * (d[0][0] + s[1][1] + s[2][2])
    xx = pressure + mu2 * d[0][0]
    yy = pressure + mu2 * s[1][1]
    zz = pressure + mu2 * s[2][2]
    xy = mu * (s[0][1] + d[1][0])
    xz = mu * (s[0][2] + d[2][0])
    yz = mu * (s[1][2] + s[2][1])
    along_y = lam3 * (d[0][1] + s[2][3])
    along_z = lam3 * (d[0][2] + s[1][3])
    along_x = lam3 * (d[1][1] + d[2][2])
    twist = mu3 * (s[0][3] + d[1][2] + d[2][1])
    fs = [
        [None, xy, xz, twist + mu3 * s[0][3]],
        [None, yy, yz, along_z + mu * s[1][3]],
        [None, yz, zz, along_y + mu * s[2][3]],
    ]
    fd = [
        [xx, along_y + mu * d[0][1], along_z + mu * d[0][2], stiff * d[0][3]],
        [xy, along_x + mu * d[1][1], twist + mu3 * d[1][2], stiff * d[1][3]],
        [xz, twist + mu3 * d[2][1], along_x + mu * d[2][2], stiff * d[2][3]],
    ]
    low = [[-fd[c][0]] + [fs[c][m] - fd[c][m] for m in range(1, 4)] for c in range(3)]
    high = [[fd[c][0]] + [fs[c][m] + fd[c][m] for m in range(1, 4)] for c in range(3)]
    return low, high


def gather_rows(modes):
    total = (modes[0] - modes[1]) + row_prev(modes[0] + modes[1])
    change = (modes[2] - modes[3]) + row_prev(modes[2] + modes[3])
    return total - change, total + change


def apply_inverse(inv, vec):
    return (
        inv[0] * vec[0] + inv[1] * vec[1] + inv[2] * vec[2],
        inv[1] * vec[0] + inv[3] * vec[1] + inv[4] * vec[2],
        inv[2] * vec[0] + inv[4] * vec[1] + inv[5] * vec[2],
    )


def block_parts(lam, mu, shift):
    stiff = lam + 4.0 * mu
    cross = lam + mu
    stiff = stiff + shift[0](stiff)
    behind = shift[1](cross)
    total = behind + cross
    change = behind - cross
    total_y = row_prev(total)
    change_y = row_prev(change)
    return (stiff + row_prev(stiff), total_y - total, change_y + change, change_y - change)


def block_inverse(before, after, valid):
    diag = (16.0 / 9.0) * (before[0] + after[0])
    p = (4.0 / 3.0) * (before[1] - after[1])
    q = (4.0 / 3.0) * (before[2] - after[2])
    s = (4.0 / 3.0) * (before[3] + after[3])
    c00 = diag * diag - s * s
    c01 = q * s - p * diag
    c02 = p * s - q * diag
    scale = 1.0 / (diag * c00 + p * c01 + q * c02)
    cof = (c00, c01, c02, diag * diag - q * q, p * q - diag * s, diag * diag - p * p)
    return [jnp.where(valid, entry * scale, 0.0) for entry in cof]


def step_weights():
    low, high = (0.3, 3.0)
    theta = (high + low) / 2.0
    delta = (high - low) / 2.0
    sigma = theta / delta
    weights = [(0.0, 1.0 / theta)]
    rho_old = 1.0 / sigma
    for _ in range(2):
        rho = 1.0 / (2.0 * sigma - rho_old)
        weights.append((rho * rho_old, 2.0 * rho / delta))
        rho_old = rho
    return weights


def smooth(
    forcing, guess, lame, shear, full, y0_near, y0_far, x_near, x_far, y1_near, y1_far,
    out_solution, out_residual,
    field, edge, strip, strip_inv, strip_step, strip_push, inv, step, modes, forces,
):
    own_fields = fields_of(forcing, guess, lame, shear)
    layers = full.shape[0]
    wide = layers + 2 * REACH
    half = layers // 2
    tall = 2 * ROWS

    y_keep = row_mask(jnp.logical_not(even("gy")))
    y_ends = at_end("gy")
    x_forward = even("gx")
    x_ends = at_end("gx")

    def scaled(f, tile):
        return tile * (1.0 / 16.0) if f in (6, 7) else tile

    def beside(near, far):
        far = jnp.where(y_ends, 0.0, far)
        return jnp.where(y_keep, near, far), half_turn(jnp.where(y_keep, far, near))

    def target(f):
        return field.at[f] if f < 8 else edge

    zero = jnp.zeros((tall, LANES), F32)
    for f in range(3, 6):
        field[f, 0] = zero
        field[f, wide - 1] = zero
    for f in range(9):
        for x in range(half):
            if f < 8:
                i = f * half + x
                first, second = beside(y0_near[i], y0_far[i])
                target(f)[REACH + x, :ROWS] = scaled(f, own_fields[f][x])
                target(f)[REACH + x + half, :ROWS] = scaled(f, own_fields[f][x + half])
            else:
                i = X_TILES + x
                first, second = beside(y1_near[i], y1_far[i])
                edge[REACH + x, :ROWS] = full[x]
                edge[REACH + x + half, :ROWS] = full[x + half]
            target(f)[REACH + x, ROWS:] = scaled(f, first)
            target(f)[REACH + x + half, ROWS:] = scaled(f, second)
    for f in range(9):
        count = X_LAYERS[f]
        ahead = REACH + layers
        behind = REACH - count
        to_near = jnp.where(x_forward, ahead, behind)
        to_far = jnp.where(x_forward, behind, ahead)
        for x in range(count):
            i = X_STARTS[f] + x
            target(f)[to_near + x, :ROWS] = scaled(f, x_near[i])
            target(f)[to_far + x, :ROWS] = jnp.where(x_ends, 0.0, scaled(f, x_far[i]))
            first, second = beside(y1_near[i], y1_far[i])
            target(f)[to_near + x, ROWS:] = scaled(f, first)
            target(f)[to_far + x, ROWS:] = jnp.where(x_ends, 0.0, scaled(f, second))

    lane = iota((tall, LANES), 1)
    row = iota((tall, LANES), 0)
    group = lax.div(lane, 16)
    slot = lax.rem(lane, 16)
    first_lane = lane == 0
    last_lane = lane == LANES - 1

    groups = wide // 3
    for i in range(3):
        for f in range(8):
            tile = zero
            for g in range(groups):
                moved = pltpu.roll(edge[3 * g + i], (16 * (g - f)) % LANES, 1)
                tile = jnp.where(group == g, moved, tile)
            strip[f, i] = scaled(f, tile)

    place_x, place_y, place_z = (lax.axis_index(axis) for axis in AXES)
    count_x, count_y, count_z = (lax.axis_size(axis) for axis in AXES)
    from_x = jnp.where(place_x == 0, REACH, 0)
    to_x = jnp.where(place_x == count_x - 1, REACH + layers, wide)
    row_from = jnp.where(place_y == count_y - 1, ROWS + 4, ROWS)
    row_to = jnp.where(place_y == 0, ROWS + 4, tall)
    row_ok = jnp.logical_or(row < ROWS, jnp.logical_and(row >= row_from, row < row_to))
    slot_from = jnp.where(place_z == 0, 4, 0)
    slot_to = jnp.where(place_z == count_z - 1, 12, 16)
    slot_ok = jnp.logical_and(row_ok, jnp.logical_and(slot >= slot_from, slot < slot_to))

    def strip_next(tiles):
        return [tiles[1], tiles[2], pltpu.roll(tiles[0], LANES - 16, 1)]

    def strip_prev(tiles):
        return [pltpu.roll(tiles[2], 16, 1), tiles[0], tiles[1]]

    def at_high(tile, g):
        return pltpu.roll(tile, lax.rem(LANES + 115 - 16 * g, LANES), 1)

    def at_low(tile, g):
        return pltpu.roll(tile, lax.rem(LANES + 125 - 16 * g, LANES), 1)

    parts = [block_parts(strip[6, i], strip[7, i], (lane_prev, lane_prev)) for i in range(3)]
    previous = [strip_prev([parts[i][k] for i in range(3)]) for k in range(4)]
    for i in range(3):
        layer = 3 * group + i
        valid = jnp.logical_and(slot_ok, jnp.logical_and(layer >= from_x, layer < to_x))
        entries = block_inverse([previous[k][i] for k in range(4)], parts[i], valid)
        for k in range(6):
            strip_inv[k, i] = entries[k]

    def main_parts(x):
        g = lax.div(x, 3)
        i = lax.rem(x, 3)
        lam_low = at_low(strip[6, i], g)
        mu_low = at_low(strip[7, i], g)

        def shift_stiff(tile):
            return jnp.where(first_lane, lam_low + 4.0 * mu_low, lane_prev(tile))

        def shift_cross(tile):
            return jnp.where(first_lane, lam_low + mu_low, lane_prev(tile))

        return block_parts(field[6, x], field[7, x], (shift_stiff, shift_cross))

    def inverse_body(x, before):
        after = main_parts(x)
        valid = jnp.logical_and(row_ok, jnp.logical_and(x >= from_x, x < to_x))
        entries = block_inverse(before, after, valid)
        for k in range(6):
            inv[k, x] = entries[k]
        return after

    lax.fori_loop(1, wide - 1, inverse_body, main_parts(0))

    weights = step_weights()
    for turn in range(4):
        final = turn == 3
        here = [[strip[c, i] for i in range(3)] for c in range(3)]
        node = [[node_modes(here[c][i], lane_next(here[c][i])) for c in range(3)] for i in range(3)]
        above = [[[None] * 4 for c in range(3)] for i in range(3)]
        for c in range(3):
            for m in range(4):
                moved = strip_next([node[i][c][m] for i in range(3)])
                for i in range(3):
                    above[i][c][m] = moved[i]
        push = [element_modes(node[i], above[i], strip[6, i], strip[7, i]) for i in range(3)]
        pull = [[None] * 3 for i in range(3)]
        for c in range(3):
            total = [[None] * 4 for i in range(3)]
            for m in range(4):
                moved = strip_prev([push[i][1][c][m] for i in range(3)])
                for i in range(3):
                    total[i][m] = moved[i] + push[i][0][c][m]
            for i in range(3):
                stay, go = gather_rows(total[i])
                strip_push[c, i] = go
                pull[i][c] = stay + lane_prev(go)

        low, high = 1 + turn, wide - 1 - turn

        def modes_body(x, carry):
            g = lax.div(x, 3)
            i = lax.rem(x, 3)
            for c in range(3):
                tile = field[c, x]
                beyond = jnp.where(last_lane, at_high(strip[c, i], g), lane_next(tile))
                for m, value in enumerate(node_modes(tile, beyond)):
                    modes[x, 4 * c + m] = value
            return carry

        lax.fori_loop(low - 1, high + 1, modes_body, 0)

        if not final:
            keep, add = weights[turn]
            for i in range(3):
                rest = [strip[3 + c, i] - pull[i][c] for c in range(3)]
                moved = apply_inverse([strip_inv[k, i] for k in range(6)], rest)
                for c in range(3):
                    change = add * moved[c]
                    if turn > 0:
                        change = keep * strip_step[c, i] + change
                    strip_step[c, i] = change
                    strip[c, i] = strip[c, i] + change

        for part in range(2):
            rows = pl.ds(part * ROWS, ROWS)

            def load_modes(x, rows=rows):
                return [[modes[x, 4 * c + m, rows] for m in range(4)] for c in range(3)]

            def forces_body(x, carry, rows=rows, load_modes=load_modes):
                lower, pushed = carry
                upper = load_modes(x + 1)
                down, up = element_modes(lower, upper, field[6, x, rows], field[7, x, rows])
                for c in range(3):
                    for m in range(4):
                        forces[x, 4 * c + m, rows] = pushed[c][m] + down[c][m]
                return upper, up

            nothing = [[jnp.zeros((ROWS, LANES), F32) for m in range(4)] for c in range(3)]
            lax.fori_loop(low - 1, high, forces_body, (load_modes(low - 1), nothing))

        def update_body(x, carry, turn=turn, final=final):
            g = lax.div(x, 3)
            i = lax.rem(x, 3)
            rest = []
            for c in range(3):
                stay, go = gather_rows([forces[x, 4 * c + m] for m in range(4)])
                come = jnp.where(first_lane, at_low(strip_push[c, i], g), lane_prev(go))
                rest.append(field[3 + c, x] - (stay + come))
            moved = apply_inverse([inv[k, x] for k in range(6)], rest)
            for c in range(3):
                if final:
                    out_residual[c, x - REACH] = moved[c][:ROWS]
                else:
                    keep, add = weights[turn]
                    change = add * moved[c]
                    if turn > 0:
                        change = keep * step[c, x] + change
                    if turn < 2:
                        step[c, x] = change
                    field[c, x] = field[c, x] + change
            return carry

        lax.fori_loop(low, high, update_body, 0)
        if turn == 2:
            for c in range(3):
                out_solution[c] = field[c, REACH : REACH + layers, :ROWS]


def vmem(count):
    return [pl.BlockSpec(memory_space=pltpu.VMEM)] * count


def tiles(*lead):
    return jax.ShapeDtypeStruct((*lead, ROWS, LANES), F32)


def solution(mesh):
    dims = tuple(mesh.shape[axis] for axis in AXES)

    def swap(value, axis, kind):
        return lax.ppermute(value, AXES, swap_pairs(dims, axis, kind))

    def body(forcing, guess, lame, shear):
        layers = lame.shape[0]
        wide = layers + 2 * REACH
        params = pltpu.CompilerParams(vmem_limit_bytes=32 * 1024 * 1024)
        own, z_near, z_far, y0_near, y0_far, x_near, x_far = pl.pallas_call(
            pack_first,
            out_shape=[tiles(layers)] + [tiles(layers // 4)] * 2 + [tiles(4 * layers)] * 2 + [tiles(X_TILES)] * 2,
            in_specs=vmem(4),
            out_specs=vmem(7),
            compiler_params=params,
            name="pack_first",
        )(forcing, guess, lame, shear)
        z_far = swap(z_far, 2, 1)
        z_near = swap(z_near, 2, 0)
        y0_near = swap(y0_near, 1, 0)
        y0_far = swap(y0_far, 1, 1)
        full, x_near, x_far = pl.pallas_call(
            pack_second,
            out_shape=[tiles(layers), tiles(X_TILES), tiles(X_TILES)],
            in_specs=vmem(5),
            out_specs=vmem(3),
            compiler_params=params,
            name="pack_second",
        )(own, z_near, z_far, x_near, x_far)
        x_near = swap(x_near, 0, 0)
        x_far = swap(x_far, 0, 1)
        y1_near, y1_far = pl.pallas_call(
            pack_third,
            out_shape=[tiles(X_TILES + layers // 2)] * 2,
            in_specs=vmem(3),
            out_specs=vmem(2),
            compiler_params=params,
            name="pack_third",
        )(full, x_near, x_far)
        y1_near = swap(y1_near, 1, 0)
        y1_far = swap(y1_far, 1, 1)
        block = (2 * ROWS, LANES)
        return pl.pallas_call(
            smooth,
            out_shape=[tiles(3, layers), tiles(3, layers)],
            in_specs=vmem(11),
            out_specs=vmem(2),
            scratch_shapes=[
                pltpu.VMEM((8, wide, *block), F32),
                pltpu.VMEM((wide, *block), F32),
                pltpu.VMEM((8, 3, *block), F32),
                pltpu.VMEM((6, 3, *block), F32),
                pltpu.VMEM((3, 3, *block), F32),
                pltpu.VMEM((3, 3, *block), F32),
                pltpu.VMEM((6, wide, *block), F32),
                pltpu.VMEM((3, wide, *block), F32),
                pltpu.VMEM((wide, 12, *block), F32),
                pltpu.VMEM((wide, 12, *block), F32),
            ],
            compiler_params=params,
            name="smooth",
        )(forcing, guess, lame, shear, full, y0_near, y0_far, x_near, x_far, y1_near, y1_far)

    in_specs = (P(None, *AXES), P(None, *AXES), P(*AXES), P(*AXES))
    out_specs = (P(None, *AXES), P(None, *AXES))
    return jax.shard_map(body, mesh=mesh, in_specs=in_specs, out_specs=out_specs, check_vma=False)
```

profile of v0, /device:TPU:160, one launch (start us, length us, event | category | flops | bytes accessed | tf_op | source)
XLA Modules:
  0.0 50.7 jit_solution(12831930166534721805)
XLA Ops:
  0.6 0.0 copy-start
  0.6 0.9 %copy-done = f32[3,16,8,128]{3,2,1,0:T(8,128)S(1)} copy-done((f32[3,16,8,128]{3,2,1,0:T(8,128)S(1)}, f32[3,16,8,128]{3,2,1,0:T(8,128)}, u32[]{:S(2)}) %copy-start) | copy-done | bytes 196632
  1.6 0.0 copy-start.2
  1.6 0.9 %copy-done.2 = f32[3,16,8,128]{3,2,1,0:T(8,128)S(1)} copy-done((f32[3,16,8,128]{3,2,1,0:T(8,128)S(1)}, f32[3,16,8,128]{3,2,1,0:T(8,128)}, u32[]{:S(2)}) %copy-start.2) | copy-done | bytes 196632
  2.5 0.0 copy-start.4
  2.5 0.8 %copy-done.4 = f32[16,8,128]{2,1,0:T(8,128)S(1)} copy-done((f32[16,8,128]{2,1,0:T(8,128)S(1)}, f32[16,8,128]{2,1,0:T(8,128)}, u32[]{:S(2)}) %copy-start.4) | copy-done | bytes 65560
  3.3 0.0 copy-start.6
  3.3 0.8 %copy-done.6 = f32[16,8,128]{2,1,0:T(8,128)S(1)} copy-done((f32[16,8,128]{2,1,0:T(8,128)S(1)}, f32[16,8,128]{2,1,0:T(8,128)}, u32[]{:S(2)}) %copy-start.6) | copy-done | bytes 65560
  4.2 0.4 pack_first.1
  4.6 0.1 collective-permute-start
  4.7 0.1 collective-permute-start.1
  4.8 1.1 %collective-permute-done.z_near = f32[4,8,128]{2,1,0:T(8,128)S(1)} collective-permute-done((f32[4,8,128]{2,1,0:T(8,128)S(1)}, f32[4,8,128]{2,1,0:T(8,128)S(1)}, u32[]{:S(2)}, u32[]{:S(2)}) %collective-permute-start) | collective-permute-done | bytes 16416 | tf_op jit(solution)/shard_map/ppermute | solution.py:499
  5.8 6.0 %collective-permute-done.1.z_far = f32[4,8,128]{2,1,0:T(8,128)S(1)} collective-permute-done((f32[4,8,128]{2,1,0:T(8,128)S(1)}, f32[4,8,128]{2,1,0:T(8,128)S(1)}, u32[]{:S(2)}, u32[]{:S(2)}) %collective-permute-start.1) | collective-permute-done | bytes 16416 | tf_op jit(solution)/shard_map/ppermute | solution.py:499
  11.8 0.0 copy-start.3
  11.8 0.1 pack_second.1
  11.9 0.0 copy-start.1
  11.9 1.6 %collective-permute-start.4 = (f32[33,8,128]{2,1,0:T(8,128)S(1)}, f32[33,8,128]{2,1,0:T(8,128)S(1)}, u32[]{:S(2)}, u32[]{:S(2)}) collective-permute-start(f32[33,8,128]{2,1,0:T(8,128)S(1)} %get-tuple-element.22), channel_id=1, source_target_pairs={{0,16},{1,17},{2,18},{3,19},{4,20},{5,21},{6,22},{7,23},{8,24},{9,... | collective-permute-start | bytes 405512 | tf_op jit(solution)/shard_map/ppermute | solution.py:499
  13.5 2.5 %collective-permute-start.5 = (f32[33,8,128]{2,1,0:T(8,128)S(1)}, f32[33,8,128]{2,1,0:T(8,128)S(1)}, u32[]{:S(2)}, u32[]{:S(2)}) collective-permute-start(f32[33,8,128]{2,1,0:T(8,128)S(1)} %get-tuple-element.23), channel_id=1, source_target_pairs={{0,4},{1,5},{2,6},{3,7},{4,0},{5,1},{6,2},{7,3},{8,12},{9,13},{10,... | collective-permute-start | bytes 405512 | tf_op jit(solution)/shard_map/ppermute | solution.py:499
  16.1 1.6 %collective-permute-start.2 = (f32[64,8,128]{2,1,0:T(8,128)S(1)}, f32[64,8,128]{2,1,0:T(8,128)S(1)}, u32[]{:S(2)}, u32[]{:S(2)}) collective-permute-start(f32[64,8,128]{2,1,0:T(8,128)S(1)} %get-tuple-element.20), channel_id=1, source_target_pairs={{0,4},{1,5},{2,6},{3,7},{4,0},{5,1},{6,2},{7,3},{8,12},{9,13},{10,... | collective-permute-start | bytes 786440 | tf_op jit(solution)/shard_map/ppermute | solution.py:499
  17.6 0.2 collective-permute-start.3
  17.8 0.7 %collective-permute-done.4.x_near = f32[33,8,128]{2,1,0:T(8,128)S(1)} collective-permute-done((f32[33,8,128]{2,1,0:T(8,128)S(1)}, f32[33,8,128]{2,1,0:T(8,128)S(1)}, u32[]{:S(2)}, u32[]{:S(2)}) %collective-permute-start.4) | collective-permute-done | bytes 135200 | tf_op jit(solution)/shard_map/ppermute | solution.py:499
  18.5 2.2 %collective-permute-done.5.x_far = f32[33,8,128]{2,1,0:T(8,128)S(1)} collective-permute-done((f32[33,8,128]{2,1,0:T(8,128)S(1)}, f32[33,8,128]{2,1,0:T(8,128)S(1)}, u32[]{:S(2)}, u32[]{:S(2)}) %collective-permute-start.5) | collective-permute-done | bytes 135200 | tf_op jit(solution)/shard_map/ppermute | solution.py:499
  20.6 0.0 copy-start.5
  20.6 0.0 copy-start.7
  20.7 1.7 %collective-permute-start.6 = (f32[41,8,128]{2,1,0:T(8,128)S(1)}, f32[41,8,128]{2,1,0:T(8,128)S(1)}, u32[]{:S(2)}, u32[]{:S(2)}) collective-permute-start(f32[41,8,128]{2,1,0:T(8,128)S(1)} %get-tuple-element.24), channel_id=1, source_target_pairs={{0,4},{1,5},{2,6},{3,7},{4,0},{5,1},{6,2},{7,3},{8,12},{9,13},{10,... | collective-permute-start | bytes 503816 | tf_op jit(solution)/shard_map/ppermute | solution.py:499
  22.3 0.0 collective-permute-start.7
  22.3 0.1 collective-permute-done.2.y0_near
  22.5 1.7 %collective-permute-done.3.y0_far = f32[64,8,128]{2,1,0:T(8,128)S(1)} collective-permute-done((f32[64,8,128]{2,1,0:T(8,128)S(1)}, f32[64,8,128]{2,1,0:T(8,128)S(1)}, u32[]{:S(2)}, u32[]{:S(2)}) %collective-permute-start.3) | collective-permute-done | bytes 262176 | tf_op jit(solution)/shard_map/ppermute | solution.py:499
  24.2 2.0 %collective-permute-done.6.y1_near = f32[41,8,128]{2,1,0:T(8,128)S(1)} collective-permute-done((f32[41,8,128]{2,1,0:T(8,128)S(1)}, f32[41,8,128]{2,1,0:T(8,128)S(1)}, u32[]{:S(2)}, u32[]{:S(2)}) %collective-permute-start.6) | collective-permute-done | bytes 167968 | tf_op jit(solution)/shard_map/ppermute | solution.py:499
  26.1 1.6 %collective-permute-done.7.y1_far = f32[41,8,128]{2,1,0:T(8,128)S(1)} collective-permute-done((f32[41,8,128]{2,1,0:T(8,128)S(1)}, f32[41,8,128]{2,1,0:T(8,128)S(1)}, u32[]{:S(2)}, u32[]{:S(2)}) %collective-permute-start.7) | collective-permute-done | bytes 167968 | tf_op jit(solution)/shard_map/ppermute | solution.py:499
  27.7 0.0 copy-done.3
  27.7 0.0 copy-done.1
  27.7 0.0 copy-done.5
  27.7 0.0 copy-done.7
  27.7 22.9 %smooth.1 = (f32[3,16,8,128]{3,2,1,0:T(8,128)}, f32[3,16,8,128]{3,2,1,0:T(8,128)}) custom-call(f32[3,16,8,128]{3,2,1,0:T(8,128)S(1)} %copy-done.1, f32[3,16,8,128]{3,2,1,0:T(8,128)S(1)} %copy-done.3, f32[16,8,128]{2,1,0:T(8,128)S(1)} %copy-done.5, f32[16,8,128]{2,1,0:T(8,128)S(1)} %copy-done.7, f32[16,8,128]{2,1,0:T(8,128)S(1)} %get-tuple-element.19.full, ...), custom_call_target="tpu_custom_call" | custom-call | tf_op jit(solution)/shard_map/smooth/pallas_call | solution.py:538
  (1 shorter events, 0.0 us)
Async XLA Ops:
  0.6 0.9 %copy-start = (f32[3,16,8,128]{3,2,1,0:T(8,128)S(1)}, f32[3,16,8,128]{3,2,1,0:T(8,128)}, u32[]{:S(2)}) copy-start(f32[3,16,8,128]{3,2,1,0:T(8,128)} %forcing.3) | copy-start | bytes 589828
  1.6 0.9 %copy-start.2 = (f32[3,16,8,128]{3,2,1,0:T(8,128)S(1)}, f32[3,16,8,128]{3,2,1,0:T(8,128)}, u32[]{:S(2)}) copy-start(f32[3,16,8,128]{3,2,1,0:T(8,128)} %guess.3) | copy-start | bytes 589828
  2.5 0.8 %copy-start.4 = (f32[16,8,128]{2,1,0:T(8,128)S(1)}, f32[16,8,128]{2,1,0:T(8,128)}, u32[]{:S(2)}) copy-start(f32[16,8,128]{2,1,0:T(8,128)} %lame.3) | copy-start | bytes 196612
  3.3 0.8 %copy-start.6 = (f32[16,8,128]{2,1,0:T(8,128)S(1)}, f32[16,8,128]{2,1,0:T(8,128)}, u32[]{:S(2)}) copy-start(f32[16,8,128]{2,1,0:T(8,128)} %shear.3) | copy-start | bytes 196612
  4.6 1.2 %collective-permute-start = (f32[4,8,128]{2,1,0:T(8,128)S(1)}, f32[4,8,128]{2,1,0:T(8,128)S(1)}, u32[]{:S(2)}, u32[]{:S(2)}) collective-permute-start(f32[4,8,128]{2,1,0:T(8,128)S(1)} %get-tuple-element.15), channel_id=1, source_target_pairs={{0,1},{1,0},{2,3},{3,2},{4,5},{5,4},{6,7},{7,6},{8,9},{9,8},{10,11... | collective-permute-start | bytes 49160 | tf_op jit(solution)/shard_map/ppermute | solution.py:499
  4.7 7.2 %collective-permute-start.1 = (f32[4,8,128]{2,1,0:T(8,128)S(1)}, f32[4,8,128]{2,1,0:T(8,128)S(1)}, u32[]{:S(2)}, u32[]{:S(2)}) collective-permute-start(f32[4,8,128]{2,1,0:T(8,128)S(1)} %get-tuple-element.16), channel_id=1, source_target_pairs={{0,4},{1,2},{2,1},{3,7},{4,0},{5,6},{6,5},{7,3},{8,12},{9,10},{10,... | collective-permute-start | bytes 49160 | tf_op jit(solution)/shard_map/ppermute | solution.py:499
  11.8 15.9 %copy-start.3 = (f32[3,16,8,128]{3,2,1,0:T(8,128)S(1)}, f32[3,16,8,128]{3,2,1,0:T(8,128)}, u32[]{:S(2)}) copy-start(f32[3,16,8,128]{3,2,1,0:T(8,128)} %guess.3) | copy-start | bytes 589828
  11.9 15.8 %copy-start.1 = (f32[3,16,8,128]{3,2,1,0:T(8,128)S(1)}, f32[3,16,8,128]{3,2,1,0:T(8,128)}, u32[]{:S(2)}) copy-start(f32[3,16,8,128]{3,2,1,0:T(8,128)} %forcing.3) | copy-start | bytes 589828
  11.9 6.5 %collective-permute-start.4 = (f32[33,8,128]{2,1,0:T(8,128)S(1)}, f32[33,8,128]{2,1,0:T(8,128)S(1)}, u32[]{:S(2)}, u32[]{:S(2)}) collective-permute-start(f32[33,8,128]{2,1,0:T(8,128)S(1)} %get-tuple-element.22), channel_id=1, source_target_pairs={{0,16},{1,17},{2,18},{3,19},{4,20},{5,21},{6,22},{7,23},{8,24},{9,... | collective-permute-start | bytes 405512 | tf_op jit(solution)/shard_map/ppermute | solution.py:499
  13.5 7.1 %collective-permute-start.5 = (f32[33,8,128]{2,1,0:T(8,128)S(1)}, f32[33,8,128]{2,1,0:T(8,128)S(1)}, u32[]{:S(2)}, u32[]{:S(2)}) collective-permute-start(f32[33,8,128]{2,1,0:T(8,128)S(1)} %get-tuple-element.23), channel_id=1, source_target_pairs={{0,4},{1,5},{2,6},{3,7},{4,0},{5,1},{6,2},{7,3},{8,12},{9,13},{10,... | collective-permute-start | bytes 405512 | tf_op jit(solution)/shard_map/ppermute | solution.py:499
  16.1 6.4 %collective-permute-start.2 = (f32[64,8,128]{2,1,0:T(8,128)S(1)}, f32[64,8,128]{2,1,0:T(8,128)S(1)}, u32[]{:S(2)}, u32[]{:S(2)}) collective-permute-start(f32[64,8,128]{2,1,0:T(8,128)S(1)} %get-tuple-element.20), channel_id=1, source_target_pairs={{0,4},{1,5},{2,6},{3,7},{4,0},{5,1},{6,2},{7,3},{8,12},{9,13},{10,... | collective-permute-start | bytes 786440 | tf_op jit(solution)/shard_map/ppermute | solution.py:499
  17.6 6.5 %collective-permute-start.3 = (f32[64,8,128]{2,1,0:T(8,128)S(1)}, f32[64,8,128]{2,1,0:T(8,128)S(1)}, u32[]{:S(2)}, u32[]{:S(2)}) collective-permute-start(f32[64,8,128]{2,1,0:T(8,128)S(1)} %get-tuple-element.21), channel_id=1, source_target_pairs={{0,16},{1,17},{2,18},{3,19},{4,8},{5,9},{6,10},{7,11},{8,4},{9,5},... | collective-permute-start | bytes 786440 | tf_op jit(solution)/shard_map/ppermute | solution.py:499
  20.6 7.1 %copy-start.5 = (f32[16,8,128]{2,1,0:T(8,128)S(1)}, f32[16,8,128]{2,1,0:T(8,128)}, u32[]{:S(2)}) copy-start(f32[16,8,128]{2,1,0:T(8,128)} %lame.3) | copy-start | bytes 196612
  20.6 7.1 %copy-start.7 = (f32[16,8,128]{2,1,0:T(8,128)S(1)}, f32[16,8,128]{2,1,0:T(8,128)}, u32[]{:S(2)}) copy-start(f32[16,8,128]{2,1,0:T(8,128)} %shear.3) | copy-start | bytes 196612
  20.7 5.4 %collective-permute-start.6 = (f32[41,8,128]{2,1,0:T(8,128)S(1)}, f32[41,8,128]{2,1,0:T(8,128)S(1)}, u32[]{:S(2)}, u32[]{:S(2)}) collective-permute-start(f32[41,8,128]{2,1,0:T(8,128)S(1)} %get-tuple-element.24), channel_id=1, source_target_pairs={{0,4},{1,5},{2,6},{3,7},{4,0},{5,1},{6,2},{7,3},{8,12},{9,13},{10,... | collective-permute-start | bytes 503816 | tf_op jit(solution)/shard_map/ppermute | solution.py:499
  22.3 5.4 %collective-permute-start.7 = (f32[41,8,128]{2,1,0:T(8,128)S(1)}, f32[41,8,128]{2,1,0:T(8,128)S(1)}, u32[]{:S(2)}, u32[]{:S(2)}) collective-permute-start(f32[41,8,128]{2,1,0:T(8,128)S(1)} %get-tuple-element.25), channel_id=1, source_target_pairs={{0,16},{1,17},{2,18},{3,19},{4,8},{5,9},{6,10},{7,11},{8,4},{9,5},... | collective-permute-start | bytes 503816 | tf_op jit(solution)/shard_map/ppermute | solution.py:499
where the time goes:
time: 50.9 us; the launch traced here: 50.7 us
  Pallas kernels  23.5 us (46%)
  waiting for transfers between devices  15.3 us (30%)
  starting transfers between devices  7.66 us (15%)
  local copies, waits for them, and re-layouts  3.54 us (7%)
  between operations  0.7 us (1%)
    pallas_call x1, Pallas kernels, body(): pl.pallas_call(smooth, out_shape=[tiles(3, layers), tiles(3, layers)], in...  22.9 us
    ppermute x8, waiting for transfers between devices, swap(): return lax.ppermute(value, AXES, swap_pairs(dims, axis, kind))  15.3 us
    ppermute x8, starting transfers between devices, swap(): return lax.ppermute(value, AXES, swap_pairs(dims, axis, kind))  7.66 us
    unnamed x16, local copies, waits for them, and re-layouts  3.54 us
  transfers between devices with their start and end apart: 8, of which 8 were waited for; matrix products, arithmetic and copies ran while one was open for 0% of the time, Pallas kernels for 0%

commit v1 on v0

--- a/solution.py
+++ b/solution.py
@@ -11,6 +11,10 @@
 REACH = 4
 F32 = jnp.float32
 LANES = 128
+TOGETHER = 6
+FIRST_TOGETHER = 8
+INVERSE_TOGETHER = 11
+FORCES_TOGETHER = 4
 ROWS = 8
 
 
@@ -63,7 +67,16 @@
 X_TILES = sum(X_LAYERS)
 
 
-def pack_first(forcing, guess, lame, shear, own, z_near, z_far, y_near, y_far, x_near, x_far):
+def pack_first(
+    forcing_hbm, guess_hbm, lame_hbm, shear_hbm, own, z_near, z_far, y_near, y_far, x_near, x_far,
+    forcing, guess, lame, shear, arrived,
+):
+    pairs = ((forcing_hbm, forcing), (guess_hbm, guess), (lame_hbm, lame), (shear_hbm, shear))
+    copies = [pltpu.make_async_copy(*pair, arrived.at[i]) for i, pair in enumerate(pairs)]
+    for copy in copies:
+        copy.start()
+    for copy in copies:
+        copy.wait()
     fields = fields_of(forcing, guess, lame, shear)
     layers = own.shape[0]
     slot = lax.rem(iota((ROWS, LANES), 1), 16)
@@ -244,6 +257,20 @@
     return [jnp.where(valid, entry * scale, 0.0) for entry in cof]
 
 
+def sweep(low, high, body, carry, together):
+    whole = (high - low) // together
+
+    def many(trip, carry):
+        for i in range(together):
+            carry = body(low + trip * together + i, carry)
+        return carry
+
+    carry = lax.fori_loop(0, whole, many, carry)
+    for x in range(low + whole * together, high):
+        carry = body(x, carry)
+    return carry
+
+
 def step_weights():
     low, high = (0.3, 3.0)
     theta = (high + low) / 2.0
@@ -386,7 +413,34 @@
             inv[k, x] = entries[k]
         return after
 
-    lax.fori_loop(1, wide - 1, inverse_body, main_parts(0))
+    sweep(1, wide - 1, inverse_body, main_parts(0), INVERSE_TOGETHER)
+
+    def place_of(x):
+        return lax.div(x, 3), lax.rem(x, 3)
+
+    def modes_of(tiles, high_edges):
+        return [
+            node_modes(tiles[c], jnp.where(last_lane, high_edges[c], lane_next(tiles[c]))) for c in range(3)
+        ]
+
+    def high_edges_of(x):
+        g, i = place_of(x)
+        return [at_high(strip[c, i], g) for c in range(3)]
+
+    def store_modes(x, values):
+        for c in range(3):
+            for m in range(4):
+                modes[x, 4 * c + m] = values[c][m]
+
+    def first_modes(trip, carry):
+        spots = [FIRST_TOGETHER * trip + i for i in range(FIRST_TOGETHER)]
+        loaded = [([field[c, x] for c in range(3)], high_edges_of(x)) for x in spots]
+        values = [modes_of(*pair) for pair in loaded]
+        for x, value in zip(spots, values):
+            store_modes(x, value)
+        return carry
+
+    lax.fori_loop(0, wide // FIRST_TOGETHER, first_modes, 0)
 
     weights = step_weights()
     for turn in range(4):
@@ -414,18 +468,6 @@
 
         low, high = 1 + turn, wide - 1 - turn
 
-        def modes_body(x, carry):
-            g = lax.div(x, 3)
-            i = lax.rem(x, 3)
-            for c in range(3):
-                tile = field[c, x]
-                beyond = jnp.where(last_lane, at_high(strip[c, i], g), lane_next(tile))
-                for m, value in enumerate(node_modes(tile, beyond)):
-                    modes[x, 4 * c + m] = value
-            return carry
-
-        lax.fori_loop(low - 1, high + 1, modes_body, 0)
-
         if not final:
             keep, add = weights[turn]
             for i in range(3):
@@ -454,31 +496,58 @@
                 return upper, up
 
             nothing = [[jnp.zeros((ROWS, LANES), F32) for m in range(4)] for c in range(3)]
-            lax.fori_loop(low - 1, high, forces_body, (load_modes(low - 1), nothing))
-
-        def update_body(x, carry, turn=turn, final=final):
-            g = lax.div(x, 3)
-            i = lax.rem(x, 3)
-            rest = []
-            for c in range(3):
-                stay, go = gather_rows([forces[x, 4 * c + m] for m in range(4)])
-                come = jnp.where(first_lane, at_low(strip_push[c, i], g), lane_prev(go))
-                rest.append(field[3 + c, x] - (stay + come))
-            moved = apply_inverse([inv[k, x] for k in range(6)], rest)
-            for c in range(3):
+            sweep(low - 1, high, forces_body, (load_modes(low - 1), nothing), FORCES_TOGETHER)
+
+        def update_layers(spots, turn=turn, final=final):
+            loaded = []
+            for x in spots:
+                g, i = place_of(x)
+                loaded.append(
+                    (
+                        [[forces[x, 4 * c + m] for m in range(4)] for c in range(3)],
+                        [at_low(strip_push[c, i], g) for c in range(3)],
+                        [field[3 + c, x] for c in range(3)],
+                        [inv[k, x] for k in range(6)],
+                        None if final else [field[c, x] for c in range(3)],
+                        [step[c, x] for c in range(3)] if 0 < turn < 3 else None,
+                        None if final else high_edges_of(x),
+                    )
+                )
+            results = []
+            for force, come, load, block, value, before, high_edges in loaded:
+                rest = []
+                for c in range(3):
+                    stay, go = gather_rows(force[c])
+                    rest.append(load[c] - (stay + jnp.where(first_lane, come[c], lane_prev(go))))
                 if final:
-                    out_residual[c, x - REACH] = moved[c][:ROWS]
-                else:
-                    keep, add = weights[turn]
-                    change = add * moved[c]
-                    if turn > 0:
-                        change = keep * step[c, x] + change
-                    if turn < 2:
-                        step[c, x] = change
-                    field[c, x] = field[c, x] + change
+                    moved = apply_inverse([entry[:ROWS] for entry in block], [part[:ROWS] for part in rest])
+                    results.append((moved, None, None))
+                    continue
+                keep, add = weights[turn]
+                moved = [add * part for part in apply_inverse(block, rest)]
+                if turn > 0:
+                    moved = [keep * before[c] + moved[c] for c in range(3)]
+                value = [value[c] + moved[c] for c in range(3)]
+                results.append((moved, value, modes_of(value, high_edges)))
+            for x, (moved, value, onward) in zip(spots, results):
+                for c in range(3):
+                    if final:
+                        out_residual[c, x - REACH] = moved[c]
+                    else:
+                        if turn < 2:
+                            step[c, x] = moved[c]
+                        field[c, x] = value[c]
+                if not final:
+                    store_modes(x, onward)
+
+        def update_body(trip, carry, low=low, update_layers=update_layers):
+            update_layers([low + TOGETHER * trip + i for i in range(TOGETHER)])
             return carry
 
-        lax.fori_loop(low, high, update_body, 0)
+        trips = (high - low) // TOGETHER
+        lax.fori_loop(0, trips, update_body, 0)
+        if low + TOGETHER * trips < high:
+            update_layers(list(range(low + TOGETHER * trips, high)))
         if turn == 2:
             for c in range(3):
                 out_solution[c] = field[c, REACH : REACH + layers, :ROWS]
@@ -505,11 +574,13 @@
         own, z_near, z_far, y0_near, y0_far, x_near, x_far = pl.pallas_call(
             pack_first,
             out_shape=[tiles(layers)] + [tiles(layers // 4)] * 2 + [tiles(4 * layers)] * 2 + [tiles(X_TILES)] * 2,
-            in_specs=vmem(4),
+            in_specs=[pl.BlockSpec(memory_space=pltpu.HBM)] * 4,
             out_specs=vmem(7),
+            scratch_shapes=[pltpu.VMEM(a.shape, F32) for a in (forcing, guess, lame, shear)]
+            + [pltpu.SemaphoreType.DMA((4,))],
             compiler_params=params,
             name="pack_first",
-        )(forcing, guess, lame, shear)
+        )(*(pltpu.with_memory_space_constraint(a, pltpu.HBM) for a in (forcing, guess, lame, shear)))
         z_far = swap(z_far, 2, 1)
         z_near = swap(z_near, 2, 0)
         y0_near = swap(y0_near, 1, 0)

time: 50.9 us -> 35.3 us (0.69)
  Pallas kernels: 23.5 us -> 11.5 us
  local copies, waits for them, and re-layouts: 3.54 us -> 0.02 us
    pallas_call x1, Pallas kernels: 22.9 us -> 9.83 us  [body(): pl.pallas_call(smooth, out_shape=[tiles(3, layers), tiles(3, layers)], in...]
    unnamed x16 -> x8, local copies, waits for them, and re-layouts: 3.54 us -> 0.02 us
    pallas_call x1, Pallas kernels: 0.42 us -> 1.52 us  [body(): pl.pallas_call(pack_first, out_shape=[tiles(layers)] + [tiles(layers // 4...]
where the time goes in v1:
time: 35.3 us; the launch traced here: 35.2 us
  waiting for transfers between devices  15.3 us (43%)
  Pallas kernels  11.5 us (33%)
  starting transfers between devices  7.7 us (22%)
  between operations  0.69 us (2%)
    ppermute x8, waiting for transfers between devices, swap(): return lax.ppermute(value, AXES, swap_pairs(dims, axis, kind))  15.3 us
    pallas_call x1, Pallas kernels, body(): pl.pallas_call(smooth, out_shape=[tiles(3, layers), tiles(3, layers)], in...  9.83 us
    ppermute x8, starting transfers between devices, swap(): return lax.ppermute(value, AXES, swap_pairs(dims, axis, kind))  7.7 us
    pallas_call x1, Pallas kernels, body(): pl.pallas_call(pack_first, out_shape=[tiles(layers)] + [tiles(layers // 4...  1.52 us
  transfers between devices with their start and end apart: 8, of which 8 were waited for; matrix products, arithmetic and copies ran while one was open for 0% of the time, Pallas kernels for 0%

profile of v1, /device:TPU:160, one launch (start us, length us, event | category | flops | bytes accessed | tf_op | source)
XLA Modules:
  0.0 35.2 jit_solution(11906819183410751644)
XLA Ops:
  0.6 1.5 %pack_first.1 = (f32[16,8,128]{2,1,0:T(8,128)S(1)}, f32[4,8,128]{2,1,0:T(8,128)S(1)}, f32[4,8,128]{2,1,0:T(8,128)S(1)}, f32[64,8,128]{2,1,0:T(8,128)S(1)}, f32[6...) custom-call(f32[3,16,8,128]{3,2,1,0:T(8,128)} %forcing.1, f32[3,16,8,128]{3,2,1,0:T(8,128)} %guess.1, ...), custom_call_target="tpu_custom_call" | custom-call | tf_op jit(solution)/shard_map/pack_first/pallas_call | solution.py:574
  2.2 0.1 collective-permute-start
  2.3 0.1 collective-permute-start.1
  2.4 1.1 %collective-permute-done.z_near = f32[4,8,128]{2,1,0:T(8,128)S(1)} collective-permute-done((f32[4,8,128]{2,1,0:T(8,128)S(1)}, f32[4,8,128]{2,1,0:T(8,128)S(1)}, u32[]{:S(2)}, u32[]{:S(2)}) %collective-permute-start) | collective-permute-done | bytes 16416 | tf_op jit(solution)/shard_map/ppermute | solution.py:568
  3.4 6.0 %collective-permute-done.1.z_far = f32[4,8,128]{2,1,0:T(8,128)S(1)} collective-permute-done((f32[4,8,128]{2,1,0:T(8,128)S(1)}, f32[4,8,128]{2,1,0:T(8,128)S(1)}, u32[]{:S(2)}, u32[]{:S(2)}) %collective-permute-start.1) | collective-permute-done | bytes 16416 | tf_op jit(solution)/shard_map/ppermute | solution.py:568
  9.4 0.0 copy-start.1
  9.4 0.1 pack_second.1
  9.5 0.0 copy-start
  9.5 1.6 %collective-permute-start.4 = (f32[33,8,128]{2,1,0:T(8,128)S(1)}, f32[33,8,128]{2,1,0:T(8,128)S(1)}, u32[]{:S(2)}, u32[]{:S(2)}) collective-permute-start(f32[33,8,128]{2,1,0:T(8,128)S(1)} %get-tuple-element.22), channel_id=1, source_target_pairs={{0,16},{1,17},{2,18},{3,19},{4,20},{5,21},{6,22},{7,23},{8,24},{9,... | collective-permute-start | bytes 405512 | tf_op jit(solution)/shard_map/ppermute | solution.py:568
  11.1 2.5 %collective-permute-start.5 = (f32[33,8,128]{2,1,0:T(8,128)S(1)}, f32[33,8,128]{2,1,0:T(8,128)S(1)}, u32[]{:S(2)}, u32[]{:S(2)}) collective-permute-start(f32[33,8,128]{2,1,0:T(8,128)S(1)} %get-tuple-element.23), channel_id=1, source_target_pairs={{0,4},{1,5},{2,6},{3,7},{4,0},{5,1},{6,2},{7,3},{8,12},{9,13},{10,... | collective-permute-start | bytes 405512 | tf_op jit(solution)/shard_map/ppermute | solution.py:568
  13.7 1.6 %collective-permute-start.2 = (f32[64,8,128]{2,1,0:T(8,128)S(1)}, f32[64,8,128]{2,1,0:T(8,128)S(1)}, u32[]{:S(2)}, u32[]{:S(2)}) collective-permute-start(f32[64,8,128]{2,1,0:T(8,128)S(1)} %get-tuple-element.20), channel_id=1, source_target_pairs={{0,4},{1,5},{2,6},{3,7},{4,0},{5,1},{6,2},{7,3},{8,12},{9,13},{10,... | collective-permute-start | bytes 786440 | tf_op jit(solution)/shard_map/ppermute | solution.py:568
  15.2 0.2 collective-permute-start.3
  15.4 0.7 %collective-permute-done.4.x_near = f32[33,8,128]{2,1,0:T(8,128)S(1)} collective-permute-done((f32[33,8,128]{2,1,0:T(8,128)S(1)}, f32[33,8,128]{2,1,0:T(8,128)S(1)}, u32[]{:S(2)}, u32[]{:S(2)}) %collective-permute-start.4) | collective-permute-done | bytes 135200 | tf_op jit(solution)/shard_map/ppermute | solution.py:568
  16.1 2.2 %collective-permute-done.5.x_far = f32[33,8,128]{2,1,0:T(8,128)S(1)} collective-permute-done((f32[33,8,128]{2,1,0:T(8,128)S(1)}, f32[33,8,128]{2,1,0:T(8,128)S(1)}, u32[]{:S(2)}, u32[]{:S(2)}) %collective-permute-start.5) | collective-permute-done | bytes 135200 | tf_op jit(solution)/shard_map/ppermute | solution.py:568
  18.2 0.0 copy-start.2
  18.2 0.0 copy-start.3
  18.3 1.7 %collective-permute-start.6 = (f32[41,8,128]{2,1,0:T(8,128)S(1)}, f32[41,8,128]{2,1,0:T(8,128)S(1)}, u32[]{:S(2)}, u32[]{:S(2)}) collective-permute-start(f32[41,8,128]{2,1,0:T(8,128)S(1)} %get-tuple-element.24), channel_id=1, source_target_pairs={{0,4},{1,5},{2,6},{3,7},{4,0},{5,1},{6,2},{7,3},{8,12},{9,13},{10,... | collective-permute-start | bytes 503816 | tf_op jit(solution)/shard_map/ppermute | solution.py:568
  19.9 0.0 collective-permute-start.7
  20.0 0.1 collective-permute-done.2.y0_near
  20.1 1.7 %collective-permute-done.3.y0_far = f32[64,8,128]{2,1,0:T(8,128)S(1)} collective-permute-done((f32[64,8,128]{2,1,0:T(8,128)S(1)}, f32[64,8,128]{2,1,0:T(8,128)S(1)}, u32[]{:S(2)}, u32[]{:S(2)}) %collective-permute-start.3) | collective-permute-done | bytes 262176 | tf_op jit(solution)/shard_map/ppermute | solution.py:568
  21.8 2.0 %collective-permute-done.6.y1_near = f32[41,8,128]{2,1,0:T(8,128)S(1)} collective-permute-done((f32[41,8,128]{2,1,0:T(8,128)S(1)}, f32[41,8,128]{2,1,0:T(8,128)S(1)}, u32[]{:S(2)}, u32[]{:S(2)}) %collective-permute-start.6) | collective-permute-done | bytes 167968 | tf_op jit(solution)/shard_map/ppermute | solution.py:568
  23.7 1.6 %collective-permute-done.7.y1_far = f32[41,8,128]{2,1,0:T(8,128)S(1)} collective-permute-done((f32[41,8,128]{2,1,0:T(8,128)S(1)}, f32[41,8,128]{2,1,0:T(8,128)S(1)}, u32[]{:S(2)}, u32[]{:S(2)}) %collective-permute-start.7) | collective-permute-done | bytes 167968 | tf_op jit(solution)/shard_map/ppermute | solution.py:568
  25.3 0.0 copy-done.1
  25.3 0.0 copy-done
  25.3 0.0 copy-done.2
  25.3 0.0 copy-done.3
  25.3 9.8 %smooth.1 = (f32[3,16,8,128]{3,2,1,0:T(8,128)}, f32[3,16,8,128]{3,2,1,0:T(8,128)}) custom-call(f32[3,16,8,128]{3,2,1,0:T(8,128)S(1)} %copy-done, f32[3,16,8,128]{3,2,1,0:T(8,128)S(1)} %copy-done.1, f32[16,8,128]{2,1,0:T(8,128)S(1)} %copy-done.2, f32[16,8,128]{2,1,0:T(8,128)S(1)} %copy-done.3, f32[16,8,128]{2,1,0:T(8,128)S(1)} %get-tuple-element.19.full, ...), custom_call_target="tpu_custom_call" | custom-call | tf_op jit(solution)/shard_map/smooth/pallas_call | solution.py:609
  (1 shorter events, 0.0 us)
Async XLA Ops:
  2.2 1.3 %collective-permute-start = (f32[4,8,128]{2,1,0:T(8,128)S(1)}, f32[4,8,128]{2,1,0:T(8,128)S(1)}, u32[]{:S(2)}, u32[]{:S(2)}) collective-permute-start(f32[4,8,128]{2,1,0:T(8,128)S(1)} %get-tuple-element.15), channel_id=1, source_target_pairs={{0,1},{1,0},{2,3},{3,2},{4,5},{5,4},{6,7},{7,6},{8,9},{9,8},{10,11... | collective-permute-start | bytes 49160 | tf_op jit(solution)/shard_map/ppermute | solution.py:568
  2.3 7.2 %collective-permute-start.1 = (f32[4,8,128]{2,1,0:T(8,128)S(1)}, f32[4,8,128]{2,1,0:T(8,128)S(1)}, u32[]{:S(2)}, u32[]{:S(2)}) collective-permute-start(f32[4,8,128]{2,1,0:T(8,128)S(1)} %get-tuple-element.16), channel_id=1, source_target_pairs={{0,4},{1,2},{2,1},{3,7},{4,0},{5,6},{6,5},{7,3},{8,12},{9,10},{10,... | collective-permute-start | bytes 49160 | tf_op jit(solution)/shard_map/ppermute | solution.py:568
  9.4 15.9 %copy-start.1 = (f32[3,16,8,128]{3,2,1,0:T(8,128)S(1)}, f32[3,16,8,128]{3,2,1,0:T(8,128)}, u32[]{:S(2)}) copy-start(f32[3,16,8,128]{3,2,1,0:T(8,128)} %guess.1) | copy-start | bytes 589828
  9.5 15.8 %copy-start = (f32[3,16,8,128]{3,2,1,0:T(8,128)S(1)}, f32[3,16,8,128]{3,2,1,0:T(8,128)}, u32[]{:S(2)}) copy-start(f32[3,16,8,128]{3,2,1,0:T(8,128)} %forcing.1) | copy-start | bytes 589828
  9.5 6.5 %collective-permute-start.4 = (f32[33,8,128]{2,1,0:T(8,128)S(1)}, f32[33,8,128]{2,1,0:T(8,128)S(1)}, u32[]{:S(2)}, u32[]{:S(2)}) collective-permute-start(f32[33,8,128]{2,1,0:T(8,128)S(1)} %get-tuple-element.22), channel_id=1, source_target_pairs={{0,16},{1,17},{2,18},{3,19},{4,20},{5,21},{6,22},{7,23},{8,24},{9,... | collective-permute-start | bytes 405512 | tf_op jit(solution)/shard_map/ppermute | solution.py:568
  11.1 7.1 %collective-permute-start.5 = (f32[33,8,128]{2,1,0:T(8,128)S(1)}, f32[33,8,128]{2,1,0:T(8,128)S(1)}, u32[]{:S(2)}, u32[]{:S(2)}) collective-permute-start(f32[33,8,128]{2,1,0:T(8,128)S(1)} %get-tuple-element.23), channel_id=1, source_target_pairs={{0,4},{1,5},{2,6},{3,7},{4,0},{5,1},{6,2},{7,3},{8,12},{9,13},{10,... | collective-permute-start | bytes 405512 | tf_op jit(solution)/shard_map/ppermute | solution.py:568
  13.7 6.4 %collective-permute-start.2 = (f32[64,8,128]{2,1,0:T(8,128)S(1)}, f32[64,8,128]{2,1,0:T(8,128)S(1)}, u32[]{:S(2)}, u32[]{:S(2)}) collective-permute-start(f32[64,8,128]{2,1,0:T(8,128)S(1)} %get-tuple-element.20), channel_id=1, source_target_pairs={{0,4},{1,5},{2,6},{3,7},{4,0},{5,1},{6,2},{7,3},{8,12},{9,13},{10,... | collective-permute-start | bytes 786440 | tf_op jit(solution)/shard_map/ppermute | solution.py:568
  15.2 6.5 %collective-permute-start.3 = (f32[64,8,128]{2,1,0:T(8,128)S(1)}, f32[64,8,128]{2,1,0:T(8,128)S(1)}, u32[]{:S(2)}, u32[]{:S(2)}) collective-permute-start(f32[64,8,128]{2,1,0:T(8,128)S(1)} %get-tuple-element.21), channel_id=1, source_target_pairs={{0,16},{1,17},{2,18},{3,19},{4,8},{5,9},{6,10},{7,11},{8,4},{9,5},... | collective-permute-start | bytes 786440 | tf_op jit(solution)/shard_map/ppermute | solution.py:568
  18.2 7.1 %copy-start.2 = (f32[16,8,128]{2,1,0:T(8,128)S(1)}, f32[16,8,128]{2,1,0:T(8,128)}, u32[]{:S(2)}) copy-start(f32[16,8,128]{2,1,0:T(8,128)} %lame.1) | copy-start | bytes 196612
  18.2 7.1 %copy-start.3 = (f32[16,8,128]{2,1,0:T(8,128)S(1)}, f32[16,8,128]{2,1,0:T(8,128)}, u32[]{:S(2)}) copy-start(f32[16,8,128]{2,1,0:T(8,128)} %shear.1) | copy-start | bytes 196612
  18.3 5.4 %collective-permute-start.6 = (f32[41,8,128]{2,1,0:T(8,128)S(1)}, f32[41,8,128]{2,1,0:T(8,128)S(1)}, u32[]{:S(2)}, u32[]{:S(2)}) collective-permute-start(f32[41,8,128]{2,1,0:T(8,128)S(1)} %get-tuple-element.24), channel_id=1, source_target_pairs={{0,4},{1,5},{2,6},{3,7},{4,0},{5,1},{6,2},{7,3},{8,12},{9,13},{10,... | collective-permute-start | bytes 503816 | tf_op jit(solution)/shard_map/ppermute | solution.py:568
  19.9 5.4 %collective-permute-start.7 = (f32[41,8,128]{2,1,0:T(8,128)S(1)}, f32[41,8,128]{2,1,0:T(8,128)S(1)}, u32[]{:S(2)}, u32[]{:S(2)}) collective-permute-start(f32[41,8,128]{2,1,0:T(8,128)S(1)} %get-tuple-element.25), channel_id=1, source_target_pairs={{0,16},{1,17},{2,18},{3,19},{4,8},{5,9},{6,10},{7,11},{8,4},{9,5},... | collective-permute-start | bytes 503816 | tf_op jit(solution)/shard_map/ppermute | solution.py:568

commit v2 on v1

--- a/solution.py
+++ b/solution.py
@@ -67,10 +67,7 @@
 X_TILES = sum(X_LAYERS)
 
 
-def pack_first(
-    forcing_hbm, guess_hbm, lame_hbm, shear_hbm, own, z_near, z_far, y_near, y_far, x_near, x_far,
-    forcing, guess, lame, shear, arrived,
-):
+def pack_first(forcing_hbm, guess_hbm, lame_hbm, shear_hbm, forcing, guess, lame, shear, own, z_near, z_far, arrived):
     pairs = ((forcing_hbm, forcing), (guess_hbm, guess), (lame_hbm, lame), (shear_hbm, shear))
     copies = [pltpu.make_async_copy(*pair, arrived.at[i]) for i, pair in enumerate(pairs)]
     for copy in copies:
@@ -104,6 +101,11 @@
             down = jnp.where(quarter == j, pltpu.roll(tile, (4 * j - 4) % LANES, 1), down)
         z_near[q] = jnp.where(up_first, up, down)
         z_far[q] = jnp.where(up_first, down, up)
+
+
+def pack_rest(forcing, guess, lame, shear, y_near, y_far, x_near, x_far):
+    fields = fields_of(forcing, guess, lame, shear)
+    layers = lame.shape[0]
     keep = row_mask(even("gy"))
     half = layers // 2
     for f in range(8):
@@ -161,12 +163,19 @@
         y_far[X_TILES + x] = jnp.where(keep, there, here)
 
 
+def turn_rows(tile, shift, seam):
+    first = pltpu.roll(tile[:ROWS], shift, 0)
+    second = pltpu.roll(tile[ROWS:], shift, 0)
+    crossing = iota((ROWS, LANES), 0) == seam
+    return jnp.concatenate([jnp.where(crossing, second, first), jnp.where(crossing, first, second)], 0)
+
+
 def row_next(tile):
-    return pltpu.roll(tile, tile.shape[0] - 1, 0)
+    return turn_rows(tile, ROWS - 1, ROWS - 1)
 
 
 def row_prev(tile):
-    return pltpu.roll(tile, 1, 0)
+    return turn_rows(tile, 1, 0)
 
 
 def lane_next(tile):
@@ -288,7 +297,7 @@
 def smooth(
     forcing, guess, lame, shear, full, y0_near, y0_far, x_near, x_far, y1_near, y1_far,
     out_solution, out_residual,
-    field, edge, strip, strip_inv, strip_step, strip_push, inv, step, modes, forces,
+    field, edge, strip, strip_inv, strip_step, strip_push, joined, inv, step, modes, forces,
 ):
     own_fields = fields_of(forcing, guess, lame, shear)
     layers = full.shape[0]
@@ -351,13 +360,21 @@
     last_lane = lane == LANES - 1
 
     groups = wide // 3
+
+    def choose(tiles):
+        chosen = tiles[0]
+        for g in range(1, groups):
+            chosen = jnp.where(group == g, tiles[g], chosen)
+        return chosen
+
     for i in range(3):
+        rows_of = [edge[3 * g + i] for g in range(groups)]
+        turned = [
+            pltpu.roll(choose([rows_of[(f + d) % groups] for f in range(8)]), 16 * d, 1) if d else choose(rows_of)
+            for d in range(groups)
+        ]
         for f in range(8):
-            tile = zero
-            for g in range(groups):
-                moved = pltpu.roll(edge[3 * g + i], (16 * (g - f)) % LANES, 1)
-                tile = jnp.where(group == g, moved, tile)
-            strip[f, i] = scaled(f, tile)
+            strip[f, i] = scaled(f, choose([turned[(g - f) % groups] for g in range(groups)]))
 
     place_x, place_y, place_z = (lax.axis_index(axis) for axis in AXES)
     count_x, count_y, count_z = (lax.axis_size(axis) for axis in AXES)
@@ -418,14 +435,36 @@
     def place_of(x):
         return lax.div(x, 3), lax.rem(x, 3)
 
-    def modes_of(tiles, high_edges):
+    def modes_of(tiles, edges):
+        beyond = [
+            jnp.where(last_lane, edges[0], lane_next(tiles[0])),
+            lane_next(jnp.where(first_lane, edges[0], tiles[1])),
+            jnp.where(last_lane, edges[1], lane_next(tiles[2])),
+        ]
+        return [node_modes(tiles[c], beyond[c]) for c in range(3)]
+
+    def pushed_along(tiles, edges):
         return [
-            node_modes(tiles[c], jnp.where(last_lane, high_edges[c], lane_next(tiles[c]))) for c in range(3)
+            jnp.where(first_lane, edges[1], lane_prev(tiles[0])),
+            lane_prev(jnp.where(last_lane, edges[2], tiles[1])),
+            jnp.where(first_lane, edges[2], lane_prev(tiles[2])),
         ]
 
-    def high_edges_of(x):
+    def join_edges(push):
+        for i in range(3):
+            joined[0, i] = jnp.where(slot == 13, pltpu.roll(strip[1, i], 1, 1), strip[0, i])
+            if push:
+                joined[1, i] = jnp.where(slot == 13, pltpu.roll(strip_push[0, i], 10, 1), strip[2, i])
+                last = pltpu.roll(strip_push[2, i], 10, 1)
+                joined[2, i] = jnp.where(slot == 13, last, pltpu.roll(strip_push[1, i], 9, 1))
+            else:
+                joined[1, i] = strip[2, i]
+
+    def edges_of(x, which):
         g, i = place_of(x)
-        return [at_high(strip[c, i], g) for c in range(3)]
+        return [at_high(joined[k, i], g) if k in which else None for k in range(3)]
+
+    join_edges(False)
 
     def store_modes(x, values):
         for c in range(3):
@@ -434,7 +473,7 @@
 
     def first_modes(trip, carry):
         spots = [FIRST_TOGETHER * trip + i for i in range(FIRST_TOGETHER)]
-        loaded = [([field[c, x] for c in range(3)], high_edges_of(x)) for x in spots]
+        loaded = [([field[c, x] for c in range(3)], edges_of(x, (0, 1))) for x in spots]
         values = [modes_of(*pair) for pair in loaded]
         for x, value in zip(spots, values):
             store_modes(x, value)
@@ -480,6 +519,8 @@
                     strip_step[c, i] = change
                     strip[c, i] = strip[c, i] + change
 
+        join_edges(True)
+
         for part in range(2):
             rows = pl.ds(part * ROWS, ROWS)
 
@@ -501,24 +542,21 @@
         def update_layers(spots, turn=turn, final=final):
             loaded = []
             for x in spots:
-                g, i = place_of(x)
                 loaded.append(
                     (
                         [[forces[x, 4 * c + m] for m in range(4)] for c in range(3)],
-                        [at_low(strip_push[c, i], g) for c in range(3)],
+                        edges_of(x, (1, 2) if final else (0, 1, 2)),
                         [field[3 + c, x] for c in range(3)],
                         [inv[k, x] for k in range(6)],
                         None if final else [field[c, x] for c in range(3)],
                         [step[c, x] for c in range(3)] if 0 < turn < 3 else None,
-                        None if final else high_edges_of(x),
                     )
                 )
             results = []
-            for force, come, load, block, value, before, high_edges in loaded:
-                rest = []
-                for c in range(3):
-                    stay, go = gather_rows(force[c])
-                    rest.append(load[c] - (stay + jnp.where(first_lane, come[c], lane_prev(go))))
+            for force, edges, load, block, value, before in loaded:
+                gathered = [gather_rows(force[c]) for c in range(3)]
+                come = pushed_along([go for stay, go in gathered], edges)
+                rest = [load[c] - (gathered[c][0] + come[c]) for c in range(3)]
                 if final:
                     moved = apply_inverse([entry[:ROWS] for entry in block], [part[:ROWS] for part in rest])
                     results.append((moved, None, None))
@@ -528,7 +566,7 @@
                 if turn > 0:
                     moved = [keep * before[c] + moved[c] for c in range(3)]
                 value = [value[c] + moved[c] for c in range(3)]
-                results.append((moved, value, modes_of(value, high_edges)))
+                results.append((moved, value, modes_of(value, edges)))
             for x, (moved, value, onward) in zip(spots, results):
                 for c in range(3):
                     if final:
@@ -571,16 +609,24 @@
         layers = lame.shape[0]
         wide = layers + 2 * REACH
         params = pltpu.CompilerParams(vmem_limit_bytes=32 * 1024 * 1024)
-        own, z_near, z_far, y0_near, y0_far, x_near, x_far = pl.pallas_call(
+        given = (forcing, guess, lame, shear)
+        *fields, own, z_near, z_far = pl.pallas_call(
             pack_first,
-            out_shape=[tiles(layers)] + [tiles(layers // 4)] * 2 + [tiles(4 * layers)] * 2 + [tiles(X_TILES)] * 2,
+            out_shape=[jax.ShapeDtypeStruct(a.shape, F32) for a in given] + [tiles(layers)] + [tiles(layers // 4)] * 2,
             in_specs=[pl.BlockSpec(memory_space=pltpu.HBM)] * 4,
             out_specs=vmem(7),
-            scratch_shapes=[pltpu.VMEM(a.shape, F32) for a in (forcing, guess, lame, shear)]
-            + [pltpu.SemaphoreType.DMA((4,))],
+            scratch_shapes=[pltpu.SemaphoreType.DMA((4,))],
             compiler_params=params,
             name="pack_first",
-        )(*(pltpu.with_memory_space_constraint(a, pltpu.HBM) for a in (forcing, guess, lame, shear)))
+        )(*(pltpu.with_memory_space_constraint(a, pltpu.HBM) for a in given))
+        y0_near, y0_far, x_near, x_far = pl.pallas_call(
+            pack_rest,
+            out_shape=[tiles(4 * layers)] * 2 + [tiles(X_TILES)] * 2,
+            in_specs=vmem(4),
+            out_specs=vmem(4),
+            compiler_params=params,
+            name="pack_rest",
+        )(*fields)
         z_far = swap(z_far, 2, 1)
         z_near = swap(z_near, 2, 0)
         y0_near = swap(y0_near, 1, 0)
@@ -618,6 +664,7 @@
                 pltpu.VMEM((6, 3, *block), F32),
                 pltpu.VMEM((3, 3, *block), F32),
                 pltpu.VMEM((3, 3, *block), F32),
+                pltpu.VMEM((3, 3, *block), F32),
                 pltpu.VMEM((6, wide, *block), F32),
                 pltpu.VMEM((3, wide, *block), F32),
                 pltpu.VMEM((wide, 12, *block), F32),
@@ -625,7 +672,7 @@
             ],
             compiler_params=params,
             name="smooth",
-        )(forcing, guess, lame, shear, full, y0_near, y0_far, x_near, x_far, y1_near, y1_far)
+        )(*fields, full, y0_near, y0_far, x_near, x_far, y1_near, y1_far)
 
     in_specs = (P(None, *AXES), P(None, *AXES), P(*AXES), P(*AXES))
     out_specs = (P(None, *AXES), P(None, *AXES))

time: 35.3 us -> 35.4 us (level)
    pallas_call x1 -> x2, Pallas kernels: 1.52 us -> 1.57 us  [the longest x1 1.5 us: body(): pl.pallas_call(pack_first, out_shape=[jax.ShapeDtypeStruct(a.shape, F32)...]
where the time goes in v2:
time: 35.4 us; the launch traced here: 35.3 us
  waiting for transfers between devices  15.2 us (43%)
  Pallas kernels  11.7 us (33%)
  starting transfers between devices  7.7 us (22%)
  between operations  0.68 us (2%)
    ppermute x8, waiting for transfers between devices, swap(): return lax.ppermute(value, AXES, swap_pairs(dims, axis, kind))  15.2 us
    pallas_call x1, Pallas kernels, body(): pl.pallas_call(smooth, out_shape=[tiles(3, layers), tiles(3, layers)], in...  10 us
    ppermute x8, starting transfers between devices, swap(): return lax.ppermute(value, AXES, swap_pairs(dims, axis, kind))  7.7 us
    pallas_call x1, Pallas kernels, body(): pl.pallas_call(pack_first, out_shape=[jax.ShapeDtypeStruct(a.shape, F32)...  1.5 us
  transfers between devices with their start and end apart: 8, of which 8 were waited for; matrix products, arithmetic and copies ran while one was open for 0% of the time, Pallas kernels for 0%

profile of v2, /device:TPU:160, one launch (start us, length us, event | category | flops | bytes accessed | tf_op | source)
XLA Modules:
  0.0 35.3 jit_solution(6510512924595440518)
XLA Ops:
  0.6 1.5 %pack_first.1 = (f32[3,16,8,128]{3,2,1,0:T(8,128)S(1)}, f32[3,16,8,128]{3,2,1,0:T(8,128)S(1)}, f32[16,8,128]{2,1,0:T(8,128)S(1)}, f32[16,8,128]{2,1,0:T(8,128)S(...) custom-call(f32[3,16,8,128]{3,2,1,0:T(8,128)} %forcing_hbm.1, ...), custom_call_target="tpu_custom_call" | custom-call | tf_op jit(solution)/shard_map/pack_first/pallas_call | solution.py:613
  2.1 0.1 collective-permute-start
  2.2 0.1 collective-permute-start.1
  2.3 0.1 pack_rest.1
  2.4 1.0 %collective-permute-done.z_near = f32[4,8,128]{2,1,0:T(8,128)S(1)} collective-permute-done((f32[4,8,128]{2,1,0:T(8,128)S(1)}, f32[4,8,128]{2,1,0:T(8,128)S(1)}, u32[]{:S(2)}, u32[]{:S(2)}) %collective-permute-start) | collective-permute-done | bytes 16416 | tf_op jit(solution)/shard_map/ppermute | solution.py:606
  3.4 6.0 %collective-permute-done.1.z_far = f32[4,8,128]{2,1,0:T(8,128)S(1)} collective-permute-done((f32[4,8,128]{2,1,0:T(8,128)S(1)}, f32[4,8,128]{2,1,0:T(8,128)S(1)}, u32[]{:S(2)}, u32[]{:S(2)}) %collective-permute-start.1) | collective-permute-done | bytes 16416 | tf_op jit(solution)/shard_map/ppermute | solution.py:606
  9.4 0.1 pack_second.1
  9.5 1.6 %collective-permute-start.4 = (f32[33,8,128]{2,1,0:T(8,128)S(1)}, f32[33,8,128]{2,1,0:T(8,128)S(1)}, u32[]{:S(2)}, u32[]{:S(2)}) collective-permute-start(f32[33,8,128]{2,1,0:T(8,128)S(1)} %get-tuple-element.30), channel_id=1, source_target_pairs={{0,16},{1,17},{2,18},{3,19},{4,20},{5,21},{6,22},{7,23},{8,24},{9,... | collective-permute-start | bytes 405512 | tf_op jit(solution)/shard_map/ppermute | solution.py:606
  11.1 2.5 %collective-permute-start.5 = (f32[33,8,128]{2,1,0:T(8,128)S(1)}, f32[33,8,128]{2,1,0:T(8,128)S(1)}, u32[]{:S(2)}, u32[]{:S(2)}) collective-permute-start(f32[33,8,128]{2,1,0:T(8,128)S(1)} %get-tuple-element.31), channel_id=1, source_target_pairs={{0,4},{1,5},{2,6},{3,7},{4,0},{5,1},{6,2},{7,3},{8,12},{9,13},{10,... | collective-permute-start | bytes 405512 | tf_op jit(solution)/shard_map/ppermute | solution.py:606
  13.6 1.6 %collective-permute-start.2 = (f32[64,8,128]{2,1,0:T(8,128)S(1)}, f32[64,8,128]{2,1,0:T(8,128)S(1)}, u32[]{:S(2)}, u32[]{:S(2)}) collective-permute-start(f32[64,8,128]{2,1,0:T(8,128)S(1)} %get-tuple-element.28), channel_id=1, source_target_pairs={{0,4},{1,5},{2,6},{3,7},{4,0},{5,1},{6,2},{7,3},{8,12},{9,13},{10,... | collective-permute-start | bytes 786440 | tf_op jit(solution)/shard_map/ppermute | solution.py:606
  15.2 0.1 collective-permute-start.3
  15.4 0.7 %collective-permute-done.4.x_near = f32[33,8,128]{2,1,0:T(8,128)S(1)} collective-permute-done((f32[33,8,128]{2,1,0:T(8,128)S(1)}, f32[33,8,128]{2,1,0:T(8,128)S(1)}, u32[]{:S(2)}, u32[]{:S(2)}) %collective-permute-start.4) | collective-permute-done | bytes 135200 | tf_op jit(solution)/shard_map/ppermute | solution.py:606
  16.0 2.2 %collective-permute-done.5.x_far = f32[33,8,128]{2,1,0:T(8,128)S(1)} collective-permute-done((f32[33,8,128]{2,1,0:T(8,128)S(1)}, f32[33,8,128]{2,1,0:T(8,128)S(1)}, u32[]{:S(2)}, u32[]{:S(2)}) %collective-permute-start.5) | collective-permute-done | bytes 135200 | tf_op jit(solution)/shard_map/ppermute | solution.py:606
  18.2 1.7 %collective-permute-start.6 = (f32[41,8,128]{2,1,0:T(8,128)S(1)}, f32[41,8,128]{2,1,0:T(8,128)S(1)}, u32[]{:S(2)}, u32[]{:S(2)}) collective-permute-start(f32[41,8,128]{2,1,0:T(8,128)S(1)} %get-tuple-element.32), channel_id=1, source_target_pairs={{0,4},{1,5},{2,6},{3,7},{4,0},{5,1},{6,2},{7,3},{8,12},{9,13},{10,... | collective-permute-start | bytes 503816 | tf_op jit(solution)/shard_map/ppermute | solution.py:606
  19.9 0.0 collective-permute-start.7
  19.9 0.1 collective-permute-done.2.y0_near
  20.0 1.7 %collective-permute-done.3.y0_far = f32[64,8,128]{2,1,0:T(8,128)S(1)} collective-permute-done((f32[64,8,128]{2,1,0:T(8,128)S(1)}, f32[64,8,128]{2,1,0:T(8,128)S(1)}, u32[]{:S(2)}, u32[]{:S(2)}) %collective-permute-start.3) | collective-permute-done | bytes 262176 | tf_op jit(solution)/shard_map/ppermute | solution.py:606
  21.7 1.9 %collective-permute-done.6.y1_near = f32[41,8,128]{2,1,0:T(8,128)S(1)} collective-permute-done((f32[41,8,128]{2,1,0:T(8,128)S(1)}, f32[41,8,128]{2,1,0:T(8,128)S(1)}, u32[]{:S(2)}, u32[]{:S(2)}) %collective-permute-start.6) | collective-permute-done | bytes 167968 | tf_op jit(solution)/shard_map/ppermute | solution.py:606
  23.7 1.6 %collective-permute-done.7.y1_far = f32[41,8,128]{2,1,0:T(8,128)S(1)} collective-permute-done((f32[41,8,128]{2,1,0:T(8,128)S(1)}, f32[41,8,128]{2,1,0:T(8,128)S(1)}, u32[]{:S(2)}, u32[]{:S(2)}) %collective-permute-start.7) | collective-permute-done | bytes 167968 | tf_op jit(solution)/shard_map/ppermute | solution.py:606
  25.3 10.0 %smooth.1 = (f32[3,16,8,128]{3,2,1,0:T(8,128)}, f32[3,16,8,128]{3,2,1,0:T(8,128)}) custom-call(f32[3,16,8,128]{3,2,1,0:T(8,128)S(1)} %get-tuple-element.18.forcing, f32[3,16,8,128]{3,2,1,0:T(8,128)S(1)} %get-tuple-element.19.guess, f32[16,8,128]{2,1,0:T(8,128)S(1)} %get-tuple-element.20.lame, f32[16,8,128]{2,1,0:T(8,128)S(1)} %get-tuple-element.21.shear, ...), custom_call_target="tpu_custom_call" | custom-call | tf_op jit(solution)/shard_map/smooth/pallas_call | solution.py:655
  (1 shorter events, 0.0 us)
Async XLA Ops:
  2.1 1.3 %collective-permute-start = (f32[4,8,128]{2,1,0:T(8,128)S(1)}, f32[4,8,128]{2,1,0:T(8,128)S(1)}, u32[]{:S(2)}, u32[]{:S(2)}) collective-permute-start(f32[4,8,128]{2,1,0:T(8,128)S(1)} %get-tuple-element.23), channel_id=1, source_target_pairs={{0,1},{1,0},{2,3},{3,2},{4,5},{5,4},{6,7},{7,6},{8,9},{9,8},{10,11... | collective-permute-start | bytes 49160 | tf_op jit(solution)/shard_map/ppermute | solution.py:606
  2.2 7.2 %collective-permute-start.1 = (f32[4,8,128]{2,1,0:T(8,128)S(1)}, f32[4,8,128]{2,1,0:T(8,128)S(1)}, u32[]{:S(2)}, u32[]{:S(2)}) collective-permute-start(f32[4,8,128]{2,1,0:T(8,128)S(1)} %get-tuple-element.24), channel_id=1, source_target_pairs={{0,4},{1,2},{2,1},{3,7},{4,0},{5,6},{6,5},{7,3},{8,12},{9,10},{10,... | collective-permute-start | bytes 49160 | tf_op jit(solution)/shard_map/ppermute | solution.py:606
  9.5 6.5 %collective-permute-start.4 = (f32[33,8,128]{2,1,0:T(8,128)S(1)}, f32[33,8,128]{2,1,0:T(8,128)S(1)}, u32[]{:S(2)}, u32[]{:S(2)}) collective-permute-start(f32[33,8,128]{2,1,0:T(8,128)S(1)} %get-tuple-element.30), channel_id=1, source_target_pairs={{0,16},{1,17},{2,18},{3,19},{4,20},{5,21},{6,22},{7,23},{8,24},{9,... | collective-permute-start | bytes 405512 | tf_op jit(solution)/shard_map/ppermute | solution.py:606
  11.1 7.1 %collective-permute-start.5 = (f32[33,8,128]{2,1,0:T(8,128)S(1)}, f32[33,8,128]{2,1,0:T(8,128)S(1)}, u32[]{:S(2)}, u32[]{:S(2)}) collective-permute-start(f32[33,8,128]{2,1,0:T(8,128)S(1)} %get-tuple-element.31), channel_id=1, source_target_pairs={{0,4},{1,5},{2,6},{3,7},{4,0},{5,1},{6,2},{7,3},{8,12},{9,13},{10,... | collective-permute-start | bytes 405512 | tf_op jit(solution)/shard_map/ppermute | solution.py:606
  13.6 6.4 %collective-permute-start.2 = (f32[64,8,128]{2,1,0:T(8,128)S(1)}, f32[64,8,128]{2,1,0:T(8,128)S(1)}, u32[]{:S(2)}, u32[]{:S(2)}) collective-permute-start(f32[64,8,128]{2,1,0:T(8,128)S(1)} %get-tuple-element.28), channel_id=1, source_target_pairs={{0,4},{1,5},{2,6},{3,7},{4,0},{5,1},{6,2},{7,3},{8,12},{9,13},{10,... | collective-permute-start | bytes 786440 | tf_op jit(solution)/shard_map/ppermute | solution.py:606
  15.2 6.5 %collective-permute-start.3 = (f32[64,8,128]{2,1,0:T(8,128)S(1)}, f32[64,8,128]{2,1,0:T(8,128)S(1)}, u32[]{:S(2)}, u32[]{:S(2)}) collective-permute-start(f32[64,8,128]{2,1,0:T(8,128)S(1)} %get-tuple-element.29), channel_id=1, source_target_pairs={{0,16},{1,17},{2,18},{3,19},{4,8},{5,9},{6,10},{7,11},{8,4},{9,5},... | collective-permute-start | bytes 786440 | tf_op jit(solution)/shard_map/ppermute | solution.py:606
  18.2 5.4 %collective-permute-start.6 = (f32[41,8,128]{2,1,0:T(8,128)S(1)}, f32[41,8,128]{2,1,0:T(8,128)S(1)}, u32[]{:S(2)}, u32[]{:S(2)}) collective-permute-start(f32[41,8,128]{2,1,0:T(8,128)S(1)} %get-tuple-element.32), channel_id=1, source_target_pairs={{0,4},{1,5},{2,6},{3,7},{4,0},{5,1},{6,2},{7,3},{8,12},{9,13},{10,... | collective-permute-start | bytes 503816 | tf_op jit(solution)/shard_map/ppermute | solution.py:606
  19.9 5.4 %collective-permute-start.7 = (f32[41,8,128]{2,1,0:T(8,128)S(1)}, f32[41,8,128]{2,1,0:T(8,128)S(1)}, u32[]{:S(2)}, u32[]{:S(2)}) collective-permute-start(f32[41,8,128]{2,1,0:T(8,128)S(1)} %get-tuple-element.33), channel_id=1, source_target_pairs={{0,16},{1,17},{2,18},{3,19},{4,8},{5,9},{6,10},{7,11},{8,4},{9,5},... | collective-permute-start | bytes 503816 | tf_op jit(solution)/shard_map/ppermute | solution.py:606

commit v3 on v2

--- a/solution.py
+++ b/solution.py
@@ -11,10 +11,10 @@
 REACH = 4
 F32 = jnp.float32
 LANES = 128
-TOGETHER = 6
-FIRST_TOGETHER = 8
+TOGETHER = 9
+FIRST_TOGETHER = 12
 INVERSE_TOGETHER = 11
-FORCES_TOGETHER = 4
+FORCES_TOGETHER = 6
 ROWS = 8
 
 
@@ -296,8 +296,8 @@
 
 def smooth(
     forcing, guess, lame, shear, full, y0_near, y0_far, x_near, x_far, y1_near, y1_far,
-    out_solution, out_residual,
-    field, edge, strip, strip_inv, strip_step, strip_push, joined, inv, step, modes, forces,
+    solution_hbm, residual_hbm,
+    out_solution, out_residual, left, field, edge, strip, strip_inv, strip_step, strip_push, joined, inv, step, modes, forces,
 ):
     own_fields = fields_of(forcing, guess, lame, shear)
     layers = full.shape[0]
@@ -481,6 +481,7 @@
 
     lax.fori_loop(0, wide // FIRST_TOGETHER, first_modes, 0)
 
+    copies = []
     weights = step_weights()
     for turn in range(4):
         final = turn == 3
@@ -584,11 +585,23 @@
 
         trips = (high - low) // TOGETHER
         lax.fori_loop(0, trips, update_body, 0)
+        if final:
+            done = pl.ds(0, TOGETHER * trips)
+            copies.append(pltpu.make_async_copy(out_residual.at[:, done], residual_hbm.at[:, done], left.at[1]))
+            copies[-1].start()
         if low + TOGETHER * trips < high:
             update_layers(list(range(low + TOGETHER * trips, high)))
+        if final and TOGETHER * trips < layers:
+            rest = pl.ds(TOGETHER * trips, layers - TOGETHER * trips)
+            copies.append(pltpu.make_async_copy(out_residual.at[:, rest], residual_hbm.at[:, rest], left.at[2]))
+            copies[-1].start()
         if turn == 2:
             for c in range(3):
                 out_solution[c] = field[c, REACH : REACH + layers, :ROWS]
+            copies.append(pltpu.make_async_copy(out_solution, solution_hbm, left.at[0]))
+            copies[-1].start()
+    for copy in copies:
+        copy.wait()
 
 
 def vmem(count):
@@ -656,8 +669,11 @@
             smooth,
             out_shape=[tiles(3, layers), tiles(3, layers)],
             in_specs=vmem(11),
-            out_specs=vmem(2),
+            out_specs=[pl.BlockSpec(memory_space=pltpu.HBM)] * 2,
             scratch_shapes=[
+                pltpu.VMEM((3, layers, ROWS, LANES), F32),
+                pltpu.VMEM((3, layers, ROWS, LANES), F32),
+                pltpu.SemaphoreType.DMA((3,)),
                 pltpu.VMEM((8, wide, *block), F32),
                 pltpu.VMEM((wide, *block), F32),
                 pltpu.VMEM((8, 3, *block), F32),

time: 35.4 us -> 34.3 us (0.969)
  Pallas kernels: 11.7 us -> 10.7 us
    pallas_call x1, Pallas kernels: 10 us -> 8.95 us  [body(): pl.pallas_call(smooth, out_shape=[tiles(3, layers), tiles(3, layers)], in...]
where the time goes in v3:
time: 34.3 us; the launch traced here: 34.2 us
  waiting for transfers between devices  15.2 us (44%)
  Pallas kernels  10.7 us (31%)
  starting transfers between devices  7.7 us (22%)
  between operations  0.68 us (2%)
    ppermute x8, waiting for transfers between devices, swap(): return lax.ppermute(value, AXES, swap_pairs(dims, axis, kind))  15.2 us
    pallas_call x1, Pallas kernels, body(): pl.pallas_call(smooth, out_shape=[tiles(3, layers), tiles(3, layers)], in...  8.95 us
    ppermute x8, starting transfers between devices, swap(): return lax.ppermute(value, AXES, swap_pairs(dims, axis, kind))  7.7 us
    pallas_call x1, Pallas kernels, body(): pl.pallas_call(pack_first, out_shape=[jax.ShapeDtypeStruct(a.shape, F32)...  1.5 us
  transfers between devices with their start and end apart: 8, of which 8 were waited for; matrix products, arithmetic and copies ran while one was open for 0% of the time, Pallas kernels for 0%

profile of v3, /device:TPU:160, one launch (start us, length us, event | category | flops | bytes accessed | tf_op | source)
XLA Modules:
  0.0 34.2 jit_solution(8376931907098818142)
XLA Ops:
  0.6 1.5 %pack_first.1 = (f32[3,16,8,128]{3,2,1,0:T(8,128)S(1)}, f32[3,16,8,128]{3,2,1,0:T(8,128)S(1)}, f32[16,8,128]{2,1,0:T(8,128)S(1)}, f32[16,8,128]{2,1,0:T(8,128)S(...) custom-call(f32[3,16,8,128]{3,2,1,0:T(8,128)} %forcing_hbm.1, ...), custom_call_target="tpu_custom_call" | custom-call | tf_op jit(solution)/shard_map/pack_first/pallas_call | solution.py:626
  2.1 0.1 collective-permute-start
  2.2 0.1 collective-permute-start.1
  2.3 0.1 pack_rest.1
  2.4 1.0 %collective-permute-done.z_near = f32[4,8,128]{2,1,0:T(8,128)S(1)} collective-permute-done((f32[4,8,128]{2,1,0:T(8,128)S(1)}, f32[4,8,128]{2,1,0:T(8,128)S(1)}, u32[]{:S(2)}, u32[]{:S(2)}) %collective-permute-start) | collective-permute-done | bytes 16416 | tf_op jit(solution)/shard_map/ppermute | solution.py:619
  3.4 6.0 %collective-permute-done.1.z_far = f32[4,8,128]{2,1,0:T(8,128)S(1)} collective-permute-done((f32[4,8,128]{2,1,0:T(8,128)S(1)}, f32[4,8,128]{2,1,0:T(8,128)S(1)}, u32[]{:S(2)}, u32[]{:S(2)}) %collective-permute-start.1) | collective-permute-done | bytes 16416 | tf_op jit(solution)/shard_map/ppermute | solution.py:619
  9.4 0.1 pack_second.1
  9.5 1.6 %collective-permute-start.4 = (f32[33,8,128]{2,1,0:T(8,128)S(1)}, f32[33,8,128]{2,1,0:T(8,128)S(1)}, u32[]{:S(2)}, u32[]{:S(2)}) collective-permute-start(f32[33,8,128]{2,1,0:T(8,128)S(1)} %get-tuple-element.30), channel_id=1, source_target_pairs={{0,16},{1,17},{2,18},{3,19},{4,20},{5,21},{6,22},{7,23},{8,24},{9,... | collective-permute-start | bytes 405512 | tf_op jit(solution)/shard_map/ppermute | solution.py:619
  11.1 2.5 %collective-permute-start.5 = (f32[33,8,128]{2,1,0:T(8,128)S(1)}, f32[33,8,128]{2,1,0:T(8,128)S(1)}, u32[]{:S(2)}, u32[]{:S(2)}) collective-permute-start(f32[33,8,128]{2,1,0:T(8,128)S(1)} %get-tuple-element.31), channel_id=1, source_target_pairs={{0,4},{1,5},{2,6},{3,7},{4,0},{5,1},{6,2},{7,3},{8,12},{9,13},{10,... | collective-permute-start | bytes 405512 | tf_op jit(solution)/shard_map/ppermute | solution.py:619
  13.6 1.6 %collective-permute-start.2 = (f32[64,8,128]{2,1,0:T(8,128)S(1)}, f32[64,8,128]{2,1,0:T(8,128)S(1)}, u32[]{:S(2)}, u32[]{:S(2)}) collective-permute-start(f32[64,8,128]{2,1,0:T(8,128)S(1)} %get-tuple-element.28), channel_id=1, source_target_pairs={{0,4},{1,5},{2,6},{3,7},{4,0},{5,1},{6,2},{7,3},{8,12},{9,13},{10,... | collective-permute-start | bytes 786440 | tf_op jit(solution)/shard_map/ppermute | solution.py:619
  15.2 0.1 collective-permute-start.3
  15.4 0.7 %collective-permute-done.4.x_near = f32[33,8,128]{2,1,0:T(8,128)S(1)} collective-permute-done((f32[33,8,128]{2,1,0:T(8,128)S(1)}, f32[33,8,128]{2,1,0:T(8,128)S(1)}, u32[]{:S(2)}, u32[]{:S(2)}) %collective-permute-start.4) | collective-permute-done | bytes 135200 | tf_op jit(solution)/shard_map/ppermute | solution.py:619
  16.0 2.2 %collective-permute-done.5.x_far = f32[33,8,128]{2,1,0:T(8,128)S(1)} collective-permute-done((f32[33,8,128]{2,1,0:T(8,128)S(1)}, f32[33,8,128]{2,1,0:T(8,128)S(1)}, u32[]{:S(2)}, u32[]{:S(2)}) %collective-permute-start.5) | collective-permute-done | bytes 135200 | tf_op jit(solution)/shard_map/ppermute | solution.py:619
  18.2 1.7 %collective-permute-start.6 = (f32[41,8,128]{2,1,0:T(8,128)S(1)}, f32[41,8,128]{2,1,0:T(8,128)S(1)}, u32[]{:S(2)}, u32[]{:S(2)}) collective-permute-start(f32[41,8,128]{2,1,0:T(8,128)S(1)} %get-tuple-element.32), channel_id=1, source_target_pairs={{0,4},{1,5},{2,6},{3,7},{4,0},{5,1},{6,2},{7,3},{8,12},{9,13},{10,... | collective-permute-start | bytes 503816 | tf_op jit(solution)/shard_map/ppermute | solution.py:619
  19.9 0.0 collective-permute-start.7
  19.9 0.1 collective-permute-done.2.y0_near
  20.0 1.7 %collective-permute-done.3.y0_far = f32[64,8,128]{2,1,0:T(8,128)S(1)} collective-permute-done((f32[64,8,128]{2,1,0:T(8,128)S(1)}, f32[64,8,128]{2,1,0:T(8,128)S(1)}, u32[]{:S(2)}, u32[]{:S(2)}) %collective-permute-start.3) | collective-permute-done | bytes 262176 | tf_op jit(solution)/shard_map/ppermute | solution.py:619
  21.7 1.9 %collective-permute-done.6.y1_near = f32[41,8,128]{2,1,0:T(8,128)S(1)} collective-permute-done((f32[41,8,128]{2,1,0:T(8,128)S(1)}, f32[41,8,128]{2,1,0:T(8,128)S(1)}, u32[]{:S(2)}, u32[]{:S(2)}) %collective-permute-start.6) | collective-permute-done | bytes 167968 | tf_op jit(solution)/shard_map/ppermute | solution.py:619
  23.7 1.6 %collective-permute-done.7.y1_far = f32[41,8,128]{2,1,0:T(8,128)S(1)} collective-permute-done((f32[41,8,128]{2,1,0:T(8,128)S(1)}, f32[41,8,128]{2,1,0:T(8,128)S(1)}, u32[]{:S(2)}, u32[]{:S(2)}) %collective-permute-start.7) | collective-permute-done | bytes 167968 | tf_op jit(solution)/shard_map/ppermute | solution.py:619
  25.3 8.9 %smooth.1 = (f32[3,16,8,128]{3,2,1,0:T(8,128)}, f32[3,16,8,128]{3,2,1,0:T(8,128)}) custom-call(f32[3,16,8,128]{3,2,1,0:T(8,128)S(1)} %get-tuple-element.18.forcing, f32[3,16,8,128]{3,2,1,0:T(8,128)S(1)} %get-tuple-element.19.guess, f32[16,8,128]{2,1,0:T(8,128)S(1)} %get-tuple-element.20.lame, f32[16,8,128]{2,1,0:T(8,128)S(1)} %get-tuple-element.21.shear, ...), custom_call_target="tpu_custom_call" | custom-call | tf_op jit(solution)/shard_map/smooth/pallas_call | solution.py:668
  (1 shorter events, 0.0 us)
Async XLA Ops:
  2.1 1.3 %collective-permute-start = (f32[4,8,128]{2,1,0:T(8,128)S(1)}, f32[4,8,128]{2,1,0:T(8,128)S(1)}, u32[]{:S(2)}, u32[]{:S(2)}) collective-permute-start(f32[4,8,128]{2,1,0:T(8,128)S(1)} %get-tuple-element.23), channel_id=1, source_target_pairs={{0,1},{1,0},{2,3},{3,2},{4,5},{5,4},{6,7},{7,6},{8,9},{9,8},{10,11... | collective-permute-start | bytes 49160 | tf_op jit(solution)/shard_map/ppermute | solution.py:619
  2.2 7.2 %collective-permute-start.1 = (f32[4,8,128]{2,1,0:T(8,128)S(1)}, f32[4,8,128]{2,1,0:T(8,128)S(1)}, u32[]{:S(2)}, u32[]{:S(2)}) collective-permute-start(f32[4,8,128]{2,1,0:T(8,128)S(1)} %get-tuple-element.24), channel_id=1, source_target_pairs={{0,4},{1,2},{2,1},{3,7},{4,0},{5,6},{6,5},{7,3},{8,12},{9,10},{10,... | collective-permute-start | bytes 49160 | tf_op jit(solution)/shard_map/ppermute | solution.py:619
  9.5 6.5 %collective-permute-start.4 = (f32[33,8,128]{2,1,0:T(8,128)S(1)}, f32[33,8,128]{2,1,0:T(8,128)S(1)}, u32[]{:S(2)}, u32[]{:S(2)}) collective-permute-start(f32[33,8,128]{2,1,0:T(8,128)S(1)} %get-tuple-element.30), channel_id=1, source_target_pairs={{0,16},{1,17},{2,18},{3,19},{4,20},{5,21},{6,22},{7,23},{8,24},{9,... | collective-permute-start | bytes 405512 | tf_op jit(solution)/shard_map/ppermute | solution.py:619
  11.1 7.1 %collective-permute-start.5 = (f32[33,8,128]{2,1,0:T(8,128)S(1)}, f32[33,8,128]{2,1,0:T(8,128)S(1)}, u32[]{:S(2)}, u32[]{:S(2)}) collective-permute-start(f32[33,8,128]{2,1,0:T(8,128)S(1)} %get-tuple-element.31), channel_id=1, source_target_pairs={{0,4},{1,5},{2,6},{3,7},{4,0},{5,1},{6,2},{7,3},{8,12},{9,13},{10,... | collective-permute-start | bytes 405512 | tf_op jit(solution)/shard_map/ppermute | solution.py:619
  13.6 6.4 %collective-permute-start.2 = (f32[64,8,128]{2,1,0:T(8,128)S(1)}, f32[64,8,128]{2,1,0:T(8,128)S(1)}, u32[]{:S(2)}, u32[]{:S(2)}) collective-permute-start(f32[64,8,128]{2,1,0:T(8,128)S(1)} %get-tuple-element.28), channel_id=1, source_target_pairs={{0,4},{1,5},{2,6},{3,7},{4,0},{5,1},{6,2},{7,3},{8,12},{9,13},{10,... | collective-permute-start | bytes 786440 | tf_op jit(solution)/shard_map/ppermute | solution.py:619
  15.2 6.5 %collective-permute-start.3 = (f32[64,8,128]{2,1,0:T(8,128)S(1)}, f32[64,8,128]{2,1,0:T(8,128)S(1)}, u32[]{:S(2)}, u32[]{:S(2)}) collective-permute-start(f32[64,8,128]{2,1,0:T(8,128)S(1)} %get-tuple-element.29), channel_id=1, source_target_pairs={{0,16},{1,17},{2,18},{3,19},{4,8},{5,9},{6,10},{7,11},{8,4},{9,5},... | collective-permute-start | bytes 786440 | tf_op jit(solution)/shard_map/ppermute | solution.py:619
  18.2 5.4 %collective-permute-start.6 = (f32[41,8,128]{2,1,0:T(8,128)S(1)}, f32[41,8,128]{2,1,0:T(8,128)S(1)}, u32[]{:S(2)}, u32[]{:S(2)}) collective-permute-start(f32[41,8,128]{2,1,0:T(8,128)S(1)} %get-tuple-element.32), channel_id=1, source_target_pairs={{0,4},{1,5},{2,6},{3,7},{4,0},{5,1},{6,2},{7,3},{8,12},{9,13},{10,... | collective-permute-start | bytes 503816 | tf_op jit(solution)/shard_map/ppermute | solution.py:619
  19.9 5.4 %collective-permute-start.7 = (f32[41,8,128]{2,1,0:T(8,128)S(1)}, f32[41,8,128]{2,1,0:T(8,128)S(1)}, u32[]{:S(2)}, u32[]{:S(2)}) collective-permute-start(f32[41,8,128]{2,1,0:T(8,128)S(1)} %get-tuple-element.33), channel_id=1, source_target_pairs={{0,16},{1,17},{2,18},{3,19},{4,8},{5,9},{6,10},{7,11},{8,4},{9,5},... | collective-permute-start | bytes 503816 | tf_op jit(solution)/shard_map/ppermute | solution.py:619

commit v4 on v3

--- a/solution.py
+++ b/solution.py
@@ -12,9 +12,9 @@
 F32 = jnp.float32
 LANES = 128
 TOGETHER = 9
-FIRST_TOGETHER = 12
-INVERSE_TOGETHER = 11
-FORCES_TOGETHER = 6
+FIRST_TOGETHER = 24
+INVERSE_TOGETHER = 22
+FORCES_TOGETHER = 12
 ROWS = 8
 
 

time: 34.3 us -> 33.4 us (0.974)
  Pallas kernels: 10.7 us -> 9.73 us
    pallas_call x1, Pallas kernels: 8.95 us -> 8.02 us  [body(): pl.pallas_call(smooth, out_shape=[tiles(3, layers), tiles(3, layers)], in...]
where the time goes in v4:
time: 33.4 us; the launch traced here: 33.3 us
  waiting for transfers between devices  15.2 us (46%)
  Pallas kernels  9.73 us (29%)
  starting transfers between devices  7.7 us (23%)
  between operations  0.68 us (2%)
    ppermute x8, waiting for transfers between devices, swap(): return lax.ppermute(value, AXES, swap_pairs(dims, axis, kind))  15.2 us
    pallas_call x1, Pallas kernels, body(): pl.pallas_call(smooth, out_shape=[tiles(3, layers), tiles(3, layers)], in...  8.02 us
    ppermute x8, starting transfers between devices, swap(): return lax.ppermute(value, AXES, swap_pairs(dims, axis, kind))  7.7 us
    pallas_call x1, Pallas kernels, body(): pl.pallas_call(pack_first, out_shape=[jax.ShapeDtypeStruct(a.shape, F32)...  1.5 us
  transfers between devices with their start and end apart: 8, of which 8 were waited for; matrix products, arithmetic and copies ran while one was open for 0% of the time, Pallas kernels for 0%

profile of v4, /device:TPU:160, one launch (start us, length us, event | category | flops | bytes accessed | tf_op | source)
XLA Modules:
  0.0 33.3 jit_solution(5360884286054398645)
XLA Ops:
  0.6 1.5 %pack_first.1 = (f32[3,16,8,128]{3,2,1,0:T(8,128)S(1)}, f32[3,16,8,128]{3,2,1,0:T(8,128)S(1)}, f32[16,8,128]{2,1,0:T(8,128)S(1)}, f32[16,8,128]{2,1,0:T(8,128)S(...) custom-call(f32[3,16,8,128]{3,2,1,0:T(8,128)} %forcing_hbm.1, ...), custom_call_target="tpu_custom_call" | custom-call | tf_op jit(solution)/shard_map/pack_first/pallas_call | solution.py:626
  2.1 0.1 collective-permute-start
  2.2 0.1 collective-permute-start.1
  2.3 0.1 pack_rest.1
  2.4 1.0 %collective-permute-done.z_near = f32[4,8,128]{2,1,0:T(8,128)S(1)} collective-permute-done((f32[4,8,128]{2,1,0:T(8,128)S(1)}, f32[4,8,128]{2,1,0:T(8,128)S(1)}, u32[]{:S(2)}, u32[]{:S(2)}) %collective-permute-start) | collective-permute-done | bytes 16416 | tf_op jit(solution)/shard_map/ppermute | solution.py:619
  3.4 6.0 %collective-permute-done.1.z_far = f32[4,8,128]{2,1,0:T(8,128)S(1)} collective-permute-done((f32[4,8,128]{2,1,0:T(8,128)S(1)}, f32[4,8,128]{2,1,0:T(8,128)S(1)}, u32[]{:S(2)}, u32[]{:S(2)}) %collective-permute-start.1) | collective-permute-done | bytes 16416 | tf_op jit(solution)/shard_map/ppermute | solution.py:619
  9.4 0.1 pack_second.1
  9.5 1.6 %collective-permute-start.4 = (f32[33,8,128]{2,1,0:T(8,128)S(1)}, f32[33,8,128]{2,1,0:T(8,128)S(1)}, u32[]{:S(2)}, u32[]{:S(2)}) collective-permute-start(f32[33,8,128]{2,1,0:T(8,128)S(1)} %get-tuple-element.30), channel_id=1, source_target_pairs={{0,16},{1,17},{2,18},{3,19},{4,20},{5,21},{6,22},{7,23},{8,24},{9,... | collective-permute-start | bytes 405512 | tf_op jit(solution)/shard_map/ppermute | solution.py:619
  11.1 2.5 %collective-permute-start.5 = (f32[33,8,128]{2,1,0:T(8,128)S(1)}, f32[33,8,128]{2,1,0:T(8,128)S(1)}, u32[]{:S(2)}, u32[]{:S(2)}) collective-permute-start(f32[33,8,128]{2,1,0:T(8,128)S(1)} %get-tuple-element.31), channel_id=1, source_target_pairs={{0,4},{1,5},{2,6},{3,7},{4,0},{5,1},{6,2},{7,3},{8,12},{9,13},{10,... | collective-permute-start | bytes 405512 | tf_op jit(solution)/shard_map/ppermute | solution.py:619
  13.6 1.6 %collective-permute-start.2 = (f32[64,8,128]{2,1,0:T(8,128)S(1)}, f32[64,8,128]{2,1,0:T(8,128)S(1)}, u32[]{:S(2)}, u32[]{:S(2)}) collective-permute-start(f32[64,8,128]{2,1,0:T(8,128)S(1)} %get-tuple-element.28), channel_id=1, source_target_pairs={{0,4},{1,5},{2,6},{3,7},{4,0},{5,1},{6,2},{7,3},{8,12},{9,13},{10,... | collective-permute-start | bytes 786440 | tf_op jit(solution)/shard_map/ppermute | solution.py:619
  15.2 0.1 collective-permute-start.3
  15.4 0.7 %collective-permute-done.4.x_near = f32[33,8,128]{2,1,0:T(8,128)S(1)} collective-permute-done((f32[33,8,128]{2,1,0:T(8,128)S(1)}, f32[33,8,128]{2,1,0:T(8,128)S(1)}, u32[]{:S(2)}, u32[]{:S(2)}) %collective-permute-start.4) | collective-permute-done | bytes 135200 | tf_op jit(solution)/shard_map/ppermute | solution.py:619
  16.0 2.2 %collective-permute-done.5.x_far = f32[33,8,128]{2,1,0:T(8,128)S(1)} collective-permute-done((f32[33,8,128]{2,1,0:T(8,128)S(1)}, f32[33,8,128]{2,1,0:T(8,128)S(1)}, u32[]{:S(2)}, u32[]{:S(2)}) %collective-permute-start.5) | collective-permute-done | bytes 135200 | tf_op jit(solution)/shard_map/ppermute | solution.py:619
  18.2 1.7 %collective-permute-start.6 = (f32[41,8,128]{2,1,0:T(8,128)S(1)}, f32[41,8,128]{2,1,0:T(8,128)S(1)}, u32[]{:S(2)}, u32[]{:S(2)}) collective-permute-start(f32[41,8,128]{2,1,0:T(8,128)S(1)} %get-tuple-element.32), channel_id=1, source_target_pairs={{0,4},{1,5},{2,6},{3,7},{4,0},{5,1},{6,2},{7,3},{8,12},{9,13},{10,... | collective-permute-start | bytes 503816 | tf_op jit(solution)/shard_map/ppermute | solution.py:619
  19.9 0.0 collective-permute-start.7
  19.9 0.1 collective-permute-done.2.y0_near
  20.0 1.7 %collective-permute-done.3.y0_far = f32[64,8,128]{2,1,0:T(8,128)S(1)} collective-permute-done((f32[64,8,128]{2,1,0:T(8,128)S(1)}, f32[64,8,128]{2,1,0:T(8,128)S(1)}, u32[]{:S(2)}, u32[]{:S(2)}) %collective-permute-start.3) | collective-permute-done | bytes 262176 | tf_op jit(solution)/shard_map/ppermute | solution.py:619
  21.7 1.9 %collective-permute-done.6.y1_near = f32[41,8,128]{2,1,0:T(8,128)S(1)} collective-permute-done((f32[41,8,128]{2,1,0:T(8,128)S(1)}, f32[41,8,128]{2,1,0:T(8,128)S(1)}, u32[]{:S(2)}, u32[]{:S(2)}) %collective-permute-start.6) | collective-permute-done | bytes 167968 | tf_op jit(solution)/shard_map/ppermute | solution.py:619
  23.7 1.6 %collective-permute-done.7.y1_far = f32[41,8,128]{2,1,0:T(8,128)S(1)} collective-permute-done((f32[41,8,128]{2,1,0:T(8,128)S(1)}, f32[41,8,128]{2,1,0:T(8,128)S(1)}, u32[]{:S(2)}, u32[]{:S(2)}) %collective-permute-start.7) | collective-permute-done | bytes 167968 | tf_op jit(solution)/shard_map/ppermute | solution.py:619
  25.3 8.0 %smooth.1 = (f32[3,16,8,128]{3,2,1,0:T(8,128)}, f32[3,16,8,128]{3,2,1,0:T(8,128)}) custom-call(f32[3,16,8,128]{3,2,1,0:T(8,128)S(1)} %get-tuple-element.18.forcing, f32[3,16,8,128]{3,2,1,0:T(8,128)S(1)} %get-tuple-element.19.guess, f32[16,8,128]{2,1,0:T(8,128)S(1)} %get-tuple-element.20.lame, f32[16,8,128]{2,1,0:T(8,128)S(1)} %get-tuple-element.21.shear, ...), custom_call_target="tpu_custom_call" | custom-call | tf_op jit(solution)/shard_map/smooth/pallas_call | solution.py:668
  (1 shorter events, 0.0 us)
Async XLA Ops:
  2.1 1.3 %collective-permute-start = (f32[4,8,128]{2,1,0:T(8,128)S(1)}, f32[4,8,128]{2,1,0:T(8,128)S(1)}, u32[]{:S(2)}, u32[]{:S(2)}) collective-permute-start(f32[4,8,128]{2,1,0:T(8,128)S(1)} %get-tuple-element.23), channel_id=1, source_target_pairs={{0,1},{1,0},{2,3},{3,2},{4,5},{5,4},{6,7},{7,6},{8,9},{9,8},{10,11... | collective-permute-start | bytes 49160 | tf_op jit(solution)/shard_map/ppermute | solution.py:619
  2.2 7.2 %collective-permute-start.1 = (f32[4,8,128]{2,1,0:T(8,128)S(1)}, f32[4,8,128]{2,1,0:T(8,128)S(1)}, u32[]{:S(2)}, u32[]{:S(2)}) collective-permute-start(f32[4,8,128]{2,1,0:T(8,128)S(1)} %get-tuple-element.24), channel_id=1, source_target_pairs={{0,4},{1,2},{2,1},{3,7},{4,0},{5,6},{6,5},{7,3},{8,12},{9,10},{10,... | collective-permute-start | bytes 49160 | tf_op jit(solution)/shard_map/ppermute | solution.py:619
  9.5 6.5 %collective-permute-start.4 = (f32[33,8,128]{2,1,0:T(8,128)S(1)}, f32[33,8,128]{2,1,0:T(8,128)S(1)}, u32[]{:S(2)}, u32[]{:S(2)}) collective-permute-start(f32[33,8,128]{2,1,0:T(8,128)S(1)} %get-tuple-element.30), channel_id=1, source_target_pairs={{0,16},{1,17},{2,18},{3,19},{4,20},{5,21},{6,22},{7,23},{8,24},{9,... | collective-permute-start | bytes 405512 | tf_op jit(solution)/shard_map/ppermute | solution.py:619
  11.1 7.1 %collective-permute-start.5 = (f32[33,8,128]{2,1,0:T(8,128)S(1)}, f32[33,8,128]{2,1,0:T(8,128)S(1)}, u32[]{:S(2)}, u32[]{:S(2)}) collective-permute-start(f32[33,8,128]{2,1,0:T(8,128)S(1)} %get-tuple-element.31), channel_id=1, source_target_pairs={{0,4},{1,5},{2,6},{3,7},{4,0},{5,1},{6,2},{7,3},{8,12},{9,13},{10,... | collective-permute-start | bytes 405512 | tf_op jit(solution)/shard_map/ppermute | solution.py:619
  13.6 6.4 %collective-permute-start.2 = (f32[64,8,128]{2,1,0:T(8,128)S(1)}, f32[64,8,128]{2,1,0:T(8,128)S(1)}, u32[]{:S(2)}, u32[]{:S(2)}) collective-permute-start(f32[64,8,128]{2,1,0:T(8,128)S(1)} %get-tuple-element.28), channel_id=1, source_target_pairs={{0,4},{1,5},{2,6},{3,7},{4,0},{5,1},{6,2},{7,3},{8,12},{9,13},{10,... | collective-permute-start | bytes 786440 | tf_op jit(solution)/shard_map/ppermute | solution.py:619
  15.2 6.5 %collective-permute-start.3 = (f32[64,8,128]{2,1,0:T(8,128)S(1)}, f32[64,8,128]{2,1,0:T(8,128)S(1)}, u32[]{:S(2)}, u32[]{:S(2)}) collective-permute-start(f32[64,8,128]{2,1,0:T(8,128)S(1)} %get-tuple-element.29), channel_id=1, source_target_pairs={{0,16},{1,17},{2,18},{3,19},{4,8},{5,9},{6,10},{7,11},{8,4},{9,5},... | collective-permute-start | bytes 786440 | tf_op jit(solution)/shard_map/ppermute | solution.py:619
  18.2 5.4 %collective-permute-start.6 = (f32[41,8,128]{2,1,0:T(8,128)S(1)}, f32[41,8,128]{2,1,0:T(8,128)S(1)}, u32[]{:S(2)}, u32[]{:S(2)}) collective-permute-start(f32[41,8,128]{2,1,0:T(8,128)S(1)} %get-tuple-element.32), channel_id=1, source_target_pairs={{0,4},{1,5},{2,6},{3,7},{4,0},{5,1},{6,2},{7,3},{8,12},{9,13},{10,... | collective-permute-start | bytes 503816 | tf_op jit(solution)/shard_map/ppermute | solution.py:619
  19.9 5.4 %collective-permute-start.7 = (f32[41,8,128]{2,1,0:T(8,128)S(1)}, f32[41,8,128]{2,1,0:T(8,128)S(1)}, u32[]{:S(2)}, u32[]{:S(2)}) collective-permute-start(f32[41,8,128]{2,1,0:T(8,128)S(1)} %get-tuple-element.33), channel_id=1, source_target_pairs={{0,16},{1,17},{2,18},{3,19},{4,8},{5,9},{6,10},{7,11},{8,4},{9,5},... | collective-permute-start | bytes 503816 | tf_op jit(solution)/shard_map/ppermute | solution.py:619
